TPU v7x, 128 devices: a whole 4x4x4 slice. The times are simulated.
128 devices in a mesh: freq: 16 (over y, x_lo, core), row: 2 (over x_hi), col: 4 (over z).
Axes of the slice: x: 4 (x_hi: 2, x_lo: 2; x = x_hi * 2 + x_lo), y: 4, z: 4, core: 2. Of those that a mesh axis runs over, the one named last changes fastest.
Arguments:
- voltages: bfloat16 [512, 256, 2048], P(('row', 'col'), 'freq'), may hold values from -6 to 6
- window: float32 [16, 2048], replicated, may hold values from -1.5 to 1.5
Outputs:
- vis_real: float32 [1024, 512, 512], P('freq', 'row', 'col')
- vis_imag: float32 [1024, 512, 512], P('freq', 'row', 'col')
All inputs are finite; a program needn't handle non-finite values.
Results may differ from a plain program's by a relative error of at most 0.007.
Values may be sent and summed in bfloat16 or wider, within the bound.
No kernel may reach another device: no remote copies, remote signals or barrier semaphores. Data moves between devices by JAX's collectives and lax.ppermute only.
A program may use at most 192 MiB of HBM per device.

v0:
```python
import math

import jax
import jax.numpy as jnp
from jax import lax
from jax.sharding import PartitionSpec as P


def from_behind(block, axis, distance):
    devices = range(lax.axis_size(axis))
    route = [(i - distance, i) for i in devices if i - distance in devices]
    return lax.ppermute(block, axis, route)


def split_table(length):
    half = length // 2
    rows = lax.broadcasted_iota(jnp.int32, (length, length), 0)
    cols = lax.broadcasted_iota(jnp.int32, (length, length), 1)
    channel = cols % half
    phase = rows * channel % length
    angle = phase.astype(jnp.float32) * (2.0 * math.pi / length)
    values = jnp.where(cols < half, jnp.cos(angle), -jnp.sin(angle))
    return (values / math.sqrt(length)).astype(jnp.bfloat16)


def arrange(turned):
    inputs_here, frames, parts, width = turned.shape
    return turned.transpose(3, 0, 2, 1).reshape(width, inputs_here, parts * frames)


def shards(voltages, window):
    in_dev, s_dev, length = voltages.shape
    taps = window.shape[0]
    half = length // 2
    following = from_behind(voltages[:, : taps - 1, :], "freq", -1)
    extended = jnp.concatenate([voltages, following], axis=1)
    total = jnp.zeros((in_dev, s_dev, length), jnp.float32)
    for k in range(taps):
        total = total + window[k][None, None, :] * extended[:, k : k + s_dev, :].astype(jnp.float32)
    filtered = total.astype(jnp.bfloat16).reshape(in_dev * s_dev, length)
    spectra = jnp.dot(filtered, split_table(length), preferred_element_type=jnp.float32)
    spectra = spectra.astype(jnp.bfloat16).reshape(in_dev, s_dev, 2, half)
    row_spectra = lax.all_gather(spectra, "col", axis=0, tiled=True)
    row_block = arrange(
        lax.all_to_all(row_spectra, "freq", split_axis=3, concat_axis=1, tiled=True)
    )
    own_block = lax.dynamic_slice_in_dim(row_block, lax.axis_index("col") * in_dev, in_dev, 1)
    column = lax.all_gather(own_block, "row", axis=1, tiled=True)
    chans, partners, depth = column.shape
    frames = depth // 2
    rotated = jnp.concatenate([-column[:, :, frames:], column[:, :, :frames]], axis=2)
    partner_all = jnp.concatenate([column, rotated], axis=1)
    products = jnp.einsum(
        "cak,cbk->cab", row_block, partner_all, preferred_element_type=jnp.float32
    )
    scale = 1.0 / frames
    return (products[:, :, :partners] * scale, products[:, :, partners:] * scale)


def solution(mesh):
    return jax.shard_map(
        shards,
        mesh=mesh,
        in_specs=(P(("row", "col"), "freq", None), P()),
        out_specs=(P("freq", "row", "col"), P("freq", "row", "col")),
        check_vma=False,
    )
```

profile of v0, /device:TPU:0, one launch (start us, length us, event | category | flops | bytes accessed | tf_op | source)
XLA Modules:
  0.0 770.1 jit_solution(5574362005302315827)
XLA Ops:
  7.2 0.0 copy-start.1
  7.2 0.0 all-gather.3.cloned.1.call-start
  7.2 0.0 copy-start
  7.2 4.6 copy.15
  11.9 1.5 collective-permute-start
  13.4 0.0 copy-done
  13.4 2.3 constant_dynamic-update-slice_fusion
  15.7 0.0 copy-done.1
  15.7 0.1 fusion.30
  15.8 69.7 %multiply_convert_fusion.6 = bf16[2048,2048]{1,0:T(8,128)(2,1)} fusion(s32[2048]{0:T(1024)S(1)} %get-tuple-element.22, s32[2048]{0:T(1024)S(1)} %get-tuple-element.23, pred[2048]{0:T(1024)(128)(4,1)S(1)} %get-tuple-element.25, pred[2048]{0:T(1024)(128)(4,1)S(1)} %get-tuple-element.24), kind=kLoop, calls=%fused_computation.12.clone.clone.clone.clone.1 | loop fusion | flops 79691776 | bytes 8409088 | tf_op jit(solution)/shard_map/dot_general | solution.py:41
  85.5 0.0 collective-permute-done
  85.5 4.2 copy_dynamic-update-slice_fusion
  89.6 43.7 %add_convert_fusion = bf16[64,16,2048]{2,1,0:T(8,128)(2,1)} fusion(bf16[64,16,2048]{2,1,0:T(8,128)(2,1)} %param.2, bf16[64,31,2048]{2,1,0:T(8,128)(2,1)} %copy_dynamic-update-slice_fusion, f32[2048]{0:T(1024)S(1)} %bitcast.46, f32[2048]{0:T(1024)S(1)} %bitcast.47, f32[2048]{0:T(1024)S(1)} %bitcast.33, f32[2048]{0:T(1024)S(1)} %bitcast.34, ...), kind=kLoop, calls=%fused_computation.23 | loop fusion | flops 100663296 | bytes 71434240 | tf_op jit(solution)/shard_map/convert_element_type | solution.py:40
  133.3 14.0 %fusion.19 = bf16[1024,2048]{1,0:T(8,128)(2,1)} fusion(bf16[1024,2048]{1,0:T(8,128)(2,1)} %bitcast.31, bf16[2048,2048]{1,0:T(8,128)(2,1)} %multiply_convert_fusion.6), kind=kOutput, calls=%fused_computation.28 | convolution fusion | flops 8592031744 | bytes 16777216 | tf_op jit(solution)/shard_map/dot_general | solution.py:41
  147.4 7.8 %reshape.30 = bf16[64,16,2,1024]{3,2,1,0:T(2,128)(2,1)} reshape(bf16[1024,2048]{1,0:T(8,128)(2,1)} %fusion.19) | data formatting | bytes 8388608 | tf_op jit(solution)/shard_map/reshape | solution.py:42
  155.1 5.6 copy.10
  160.8 0.0 all-gather.3.cloned.1.call-update
  160.8 158.0 %all-gather.3.cloned.1.call-done = bf16[256,16,2,1024]{3,1,2,0:T(8,128)(2,1)} async-done(((bf16[64,16,2,1024]{3,1,2,0:T(8,128)(2,1)}), bf16[256,16,2,1024]{3,1,2,0:T(8,128)(2,1)}) %all-gather.3.cloned.1.call-update) | async-done | bytes 16777232 | tf_op jit(solution)/shard_map/all_gather | solution.py:43
  318.8 32.3 %copy.11 = bf16[256,16,2,1024]{0,2,1,3:T(2,128)(2,1)} copy(bf16[256,16,2,1024]{3,1,2,0:T(8,128)(2,1)} %all-gather.3.cloned.1.call-done) | data formatting | bytes 33554432 | tf_op jit(solution)/shard_map/all_gather | solution.py:43
  351.1 5.3 all-to-all-start
  356.5 0.0 all-gather.5.cloned.1.call-start
  356.5 185.2 %all-to-all-done = bf16[256,16,2,1024]{0,2,1,3:T(2,128)(2,1)} async-done(((bf16[256,16,2,1024]{0,2,1,3:T(2,128)(2,1)}), bf16[256,16,2,1024]{0,2,1,3:T(2,128)(2,1)}, u32[]{:S(2)}, u32[]{:S(2)}) %all-to-all-start) | async-done | bytes 16777248 | tf_op jit(solution)/shard_map/all_to_all | solution.py:45
  541.7 10.1 %copy.12 = bf16[256,16,2,1024]{0,3,2,1:T(8,128)(2,1)S(1)} copy(bf16[256,16,2,1024]{0,2,1,3:T(2,128)(2,1)} %all-to-all-done) | data formatting | bytes 33554432 | tf_op jit(solution)/shard_map/all_to_all | solution.py:45
  551.8 6.5 copy.13
  558.3 30.2 %copy.14 = bf16[64,256,2,256]{3,2,1,0:T(2,128)(2,1)} copy(bf16[64,256,2,256]{1,0,2,3:T(8,128)(2,1)} %bitcast.29) | data formatting | bytes 33554432 | tf_op jit(solution)/shard_map/transpose | solution.py:28
  588.5 26.9 %reshape.31 = bf16[64,256,512]{2,1,0:T(8,128)(2,1)} reshape(bf16[64,256,2,256]{3,2,1,0:T(2,128)(2,1)} %copy.14) | data formatting | bytes 33554432 | tf_op jit(solution)/shard_map/reshape | solution.py:28
  615.4 4.7 constant_dynamic-slice_fusion
  620.1 0.0 all-gather.5.cloned.1.call-update
  620.2 107.4 %all-gather.5.cloned.1.call-done = bf16[64,128,512]{2,1,0:T(8,128)(2,1)} async-done(((bf16[64,64,512]{2,1,0:T(8,128)(2,1)}), bf16[64,128,512]{2,1,0:T(8,128)(2,1)}) %all-gather.5.cloned.1.call-update) | async-done | bytes 8388624 | tf_op jit(solution)/shard_map/all_gather | solution.py:48
  727.6 5.8 slice_negate_fusion
  733.4 19.0 %fusion.3 = f32[64,256,256]{2,1,0:T(8,128)} fusion(bf16[64,256,512]{2,1,0:T(8,128)(2,1)} %reshape.31, bf16[64,128,256]{2,1,0:T(8,128)(2,1)} %get-tuple-element.5, bf16[64,128,256]{2,1,0:T(8,128)(2,1)} %get-tuple-element.4, bf16[64,128,512]{2,1,0:T(8,128)(2,1)} %all-gather.5.cloned.1.call-done), kind=kOutput, calls=%fused_computation.6 | convolution fusion | flops 4345298944 | bytes 50331648 | tf_op jit(solution)/shard_map/cak,cbk->cab/dot_general | solution.py:53
  752.4 10.8 %slice_multiply_fusion = (f32[64,256,128]{2,1,0:T(8,128)}, f32[64,256,128]{2,1,0:T(8,128)}) fusion(f32[64,256,256]{2,1,0:T(8,128)} %fusion.3), kind=kLoop, calls=%fused_computation.14 | loop fusion | flops 4194304 | bytes 33554432 | tf_op jit(solution)/shard_map/mul | solution.py:57
  (2 shorter events, 0.0 us)
Async XLA Ops:
  7.2 8.5 %copy-start.1 = (f32[16,2048]{1,0:T(8,128)S(1)}, f32[16,2048]{1,0:T(8,128)}, u32[]{:S(2)}) copy-start(f32[16,2048]{1,0:T(8,128)} %param.3) | copy-start | bytes 393220
  7.2 311.7 %all-gather.3.cloned.1.call-start = ((), (), s32[]{:S(2)}) async-start(), calls=%async_computation.1 | async-start | bytes 20971520 | tf_op jit(solution)/shard_map/all_gather | solution.py:43
  7.2 6.2 copy-start
  11.9 73.6 %collective-permute-start = (bf16[64,15,2048]{2,0,1:T(8,128)(2,1)S(1)}, bf16[64,15,2048]{2,0,1:T(8,128)(2,1)S(1)}, u32[]{:S(2)}, u32[]{:S(2)}) collective-permute-start(bf16[64,15,2048]{2,0,1:T(8,128)(2,1)S(1)} %copy.15), channel_id=1, source_target_pairs={{8,0},{16,8},{24,16},{32,24},{40,32},{48,40},{56,48},{64,56},{72,6... | collective-permute-start | bytes 11796488 | tf_op jit(solution)/shard_map/ppermute | solution.py:12
  351.1 190.6 %all-to-all-start = ((bf16[256,16,2,1024]{0,2,1,3:T(2,128)(2,1)}), bf16[256,16,2,1024]{0,2,1,3:T(2,128)(2,1)}, u32[]{:S(2)}, u32[]{:S(2)}) async-start(bf16[256,16,2,1024]{0,2,1,3:T(2,128)(2,1)} %copy.11), calls=%async_computation | async-start | bytes 33554432 | tf_op jit(solution)/shard_map/all_to_all | solution.py:45
  356.5 371.1 %all-gather.5.cloned.1.call-start = ((), (), s32[]{:S(2)}) async-start(), calls=%async_computation.2 | async-start | bytes 12582912 | tf_op jit(solution)/shard_map/all_gather | solution.py:48
Sparse Core Ops, SparseCore 0:
  160.9 157.8 all-gather.2
  620.3 107.2 all-gather.4
where the time goes:
time: 773 us; the launch traced here: 770 us
  waiting for transfers between devices  451 us (58%)
  local copies, waits for them, and re-layouts  135 us (17%)
  other arithmetic  130 us (17%)
  matrix products  33 us (4%)
  between operations  14.1 us (2%)
    all_to_all x1, waiting for transfers between devices, shards(): lax.all_to_all(row_spectra, 'freq', split_axis=3, concat_axis=1, tiled=True)  185 us
    all_gather x1, waiting for transfers between devices, shards(): row_spectra = lax.all_gather(spectra, 'col', axis=0, tiled=True)  158 us
    all_gather x1, waiting for transfers between devices, shards(): column = lax.all_gather(own_block, 'row', axis=1, tiled=True)  107 us
    dot_general x1, other arithmetic, shards(): jnp.dot(filtered, split_table(length), preferred_element_type=jnp.float32)  69.7 us
    convert_element_type x1, other arithmetic, shards(): filtered = total.astype(jnp.bfloat16).reshape(in_dev * s_dev, length)  43.7 us
    all_gather x1, local copies, waits for them, and re-layouts, shards(): row_spectra = lax.all_gather(spectra, 'col', axis=0, tiled=True)  32.3 us
    transpose x1, local copies, waits for them, and re-layouts, arrange(): turned.transpose(3, 0, 2, 1).reshape(width, inputs_here, parts * frames)  30.2 us
    reshape x1, local copies, waits for them, and re-layouts, arrange(): turned.transpose(3, 0, 2, 1).reshape(width, inputs_here, parts * frames)  26.9 us
  transfers between devices with their start and end apart: 4, of which 3 were waited for; matrix products, arithmetic and copies ran while one was open for 9% of the time, Pallas kernels for 0%

commit v1 on v0

v1 whole, which is shorter than its diff:
```python
import functools
import math

import jax
import jax.numpy as jnp
import ml_dtypes
import numpy as np
from jax import lax
from jax.experimental import pallas as pl
from jax.experimental.pallas import tpu as pltpu
from jax.sharding import PartitionSpec as P

LANES = 128
CHUNKS = 4
COLS = 256


def dft_table(length, groups):
    half = length // 2
    width = half // groups
    base = np.arange(length) * (2.0 * math.pi / length)
    cosine = np.cos(base) / math.sqrt(length)
    sine = -np.sin(base) / math.sqrt(length)
    phase = np.arange(length)[:, None] * np.arange(half)[None, :] % length
    parts = np.stack([cosine[phase], sine[phase]], axis=1)
    parts = parts.reshape(length, 2, groups, width).transpose(2, 0, 1, 3)
    blocks = parts.reshape(groups // 2, 2, length, 2 * width).transpose(0, 2, 1, 3)
    return blocks.reshape(groups // 2, length, 4 * width).astype(ml_dtypes.bfloat16)


def channelize_kernel(v_ref, h_ref, w_ref, t_ref, u_ref, ext, acc, filt):
    n_in, frames, length = v_ref.shape
    taps = w_ref.shape[0]
    depth = 2 * frames

    @pl.when(pl.program_id(0) == 0)
    def _():
        def one_tile(t, carry):
            lanes = pl.ds(pl.multiple_of(t * LANES, LANES), LANES)
            for i in range(n_in):
                ext[pl.ds(i * depth, frames), :] = v_ref[i, :, lanes].astype(jnp.float32)
                ext[pl.ds(i * depth + frames, frames), :] = h_ref[i, :, lanes].astype(jnp.float32)
            weights = [w_ref[pl.ds(k, 1), lanes] for k in range(taps)]
            weights = [jnp.broadcast_to(w, (8, LANES)) for w in weights]
            for g in range(n_in // 8):
                x = [ext[pl.ds(g * 8 * depth + s, 8, stride=depth), :] for s in range(frames + taps - 1)]
                for s in range(frames):
                    total = weights[0] * x[s]
                    for k in range(1, taps):
                        total = total + weights[k] * x[s + k]
                    acc[pl.ds(g * 8 * frames + s, 8, stride=frames), :] = total
            filt[:, lanes] = acc[...].astype(jnp.bfloat16)
            return carry

        lax.fori_loop(0, length // LANES, one_tile, 0)

    out = jnp.dot(filt[...], t_ref[0], preferred_element_type=jnp.float32)
    out = out.astype(jnp.bfloat16)
    for j in range(u_ref.shape[0]):
        u_ref[j] = out[:, j * LANES : (j + 1) * LANES].reshape(n_in, frames, LANES)


def channelize(chunk, n_in, voltages, halo, window, table):
    frames, length = voltages.shape[1:]
    blocks = table.shape[0]
    groups = 2 * blocks
    rows = n_in * frames
    return pl.pallas_call(
        channelize_kernel,
        grid=(blocks,),
        in_specs=[
            pl.BlockSpec((n_in, frames, length), lambda b: (chunk, 0, 0)),
            pl.BlockSpec((n_in, frames, length), lambda b: (0, 0, 0)),
            pl.BlockSpec(window.shape, lambda b: (0, 0)),
            pl.BlockSpec((1, length, COLS), lambda b: (b, 0, 0)),
        ],
        out_specs=pl.BlockSpec((2, n_in, frames, LANES), lambda b: (b, 0, 0, 0)),
        out_shape=jax.ShapeDtypeStruct((groups, n_in, frames, LANES), jnp.bfloat16),
        scratch_shapes=[
            pltpu.VMEM((2 * rows, LANES), jnp.float32),
            pltpu.VMEM((rows, LANES), jnp.float32),
            pltpu.VMEM((rows, length), jnp.bfloat16),
        ],
        compiler_params=pltpu.CompilerParams(vmem_limit_bytes=32 * 2**20),
        cost_estimate=pl.CostEstimate(
            flops=2 * rows * length * length, bytes_accessed=12 * 2**20, transcendentals=0
        ),
        name="channelize",
    )(voltages, halo, window, table)


def turn_kernel(x_ref, g_ref, scr):
    devices, n_in, frames, lanes = x_ref.shape
    chans = lanes // 2
    depth = devices * frames
    for i in range(n_in):
        block = x_ref[:, i, :, :].reshape(depth, lanes).astype(jnp.float32)
        for h in range(depth // LANES):
            piece = block[h * LANES : (h + 1) * LANES, :].T
            scr[h, pl.ds(i, chans, stride=2 * n_in), :] = piece[:chans]
            scr[h, pl.ds(n_in + i, chans, stride=2 * n_in), :] = piece[chans:]
    for h in range(depth // LANES):
        g_ref[:, :, h * LANES : (h + 1) * LANES] = (
            scr[h].reshape(chans, 2 * n_in, LANES).astype(jnp.bfloat16)
        )


def turn(received):
    devices, n_in, frames, lanes = received.shape
    chans, depth = lanes // 2, devices * frames
    return pl.pallas_call(
        turn_kernel,
        out_shape=jax.ShapeDtypeStruct((chans, 2 * n_in, depth), jnp.bfloat16),
        scratch_shapes=[pltpu.VMEM((depth // LANES, chans * 2 * n_in, LANES), jnp.float32)],
        compiler_params=pltpu.CompilerParams(vmem_limit_bytes=32 * 2**20),
        cost_estimate=pl.CostEstimate(flops=10**9, bytes_accessed=4 * 2**20, transcendentals=0),
        name="turn",
    )(received)


def correlate_kernel(chunks, scale, place, *refs):
    blocks = refs[: 4 * chunks]
    swapped = refs[4 * chunks : 5 * chunks]
    re_ref, im_ref, partner = refs[5 * chunks :]
    chans, twice, depth = blocks[0].shape
    n_in = twice // 2
    inputs = n_in * chunks
    half = partner.shape[0] // 2
    for ch in range(chans):
        for row in range(2):

            @pl.when(place[0] == row)
            def _(own_at=row * inputs, far_at=(1 - row) * inputs):
                for q in range(chunks):
                    near, far = blocks[q][ch], swapped[q][ch]
                    at = q * n_in
                    partner[own_at + at : own_at + at + n_in, :] = near[:n_in]
                    partner[half + own_at + at : half + own_at + at + n_in, :] = near[n_in:]
                    partner[far_at + at : far_at + at + n_in, :] = far[:n_in]
                    partner[half + far_at + at : half + far_at + at + n_in, :] = far[n_in:]

        first = jnp.concatenate([ref[ch] for ref in blocks], axis=0)
        products = lax.dot_general(
            first, partner[...], (((1,), (1,)), ((), ())), preferred_element_type=jnp.float32
        )
        for d in range(4):
            at = pl.multiple_of(place[1 + d] * inputs, inputs)
            for q in range(chunks):
                start = (d * chunks + q) * twice
                re = products[start : start + n_in]
                im = products[start + n_in : start + twice]
                rows = pl.ds(at + q * n_in, n_in)
                re_ref[ch, rows, :] = (re[:, :half] + im[:, half:]) * scale
                im_ref[ch, rows, :] = (im[:, :half] - re[:, half:]) * scale


def correlate(place, blocks, swapped, step=4):
    chunks = len(swapped)
    chans, twice, depth = swapped[0].shape
    inputs = twice // 2 * chunks
    spec = pl.BlockSpec((step, twice, depth), lambda b, place: (b, 0, 0))
    out = pl.BlockSpec((step, 4 * inputs, 2 * inputs), lambda b, place: (b, 0, 0))
    shape = jax.ShapeDtypeStruct((chans, 4 * inputs, 2 * inputs), jnp.float32)
    return pl.pallas_call(
        functools.partial(correlate_kernel, chunks, 1.0 / depth),
        grid_spec=pltpu.PrefetchScalarGridSpec(
            num_scalar_prefetch=1,
            grid=(chans // step,),
            in_specs=[spec] * (5 * chunks),
            out_specs=[out, out],
            scratch_shapes=[pltpu.VMEM((4 * inputs, depth), jnp.bfloat16)],
        ),
        out_shape=[shape, shape],
        compiler_params=pltpu.CompilerParams(vmem_limit_bytes=40 * 2**20),
        cost_estimate=pl.CostEstimate(
            flops=2 * chans * 8 * inputs * 4 * inputs * depth,
            bytes_accessed=36 * 2**20,
            transcendentals=0,
        ),
        name="correlate",
    )(place, *blocks, *swapped)


def ring(size, distance):
    return [(i, (i + distance) % size) for i in range(size)]


def shards(voltages, window, table):
    in_dev, frames, length = voltages.shape
    n_freq, n_col = lax.axis_size("freq"), lax.axis_size("col")
    n_in = in_dev // CHUNKS
    back = [(i + 1, i) for i in range(n_freq - 1)]
    row, col = lax.axis_index("row"), lax.axis_index("col")
    up, down = ring(n_col, 1), ring(n_col, -1)
    own, below, above, across, swapped = [], [], [], [], []
    for q in range(CHUNKS):
        halo = lax.ppermute(voltages[q * n_in : (q + 1) * n_in], "freq", back)
        sent = channelize(q, n_in, voltages, halo, window, table)
        received = lax.all_to_all(sent, "freq", split_axis=0, concat_axis=0, tiled=True)
        block = turn(received)
        own.append(block)
        below.append(lax.ppermute(block, "col", up))
        above.append(lax.ppermute(block, "col", down))
        if q % 2 == 0:
            across.append(lax.ppermute(below[-1], "col", up))
        else:
            across.append(lax.ppermute(above[-1], "col", down))
        swapped.append(lax.ppermute(block, "row", ring(2, 1)))
    place = jnp.stack([row, col, (col + 3) % 4, (col + 1) % 4, (col + 2) % 4]).astype(jnp.int32)
    return tuple(correlate(place, own + below + above + across, swapped))


def solution(mesh):
    n_freq = mesh.shape["freq"]

    def run(voltages, window):
        table = jnp.asarray(dft_table(voltages.shape[2], n_freq))
        return jax.shard_map(
            shards,
            mesh=mesh,
            in_specs=(P(("row", "col"), "freq", None), P(), P()),
            out_specs=(P("freq", "row", "col"), P("freq", "row", "col")),
            check_vma=False,
        )(voltages, window, table)

    return run
```

time: 773 us -> 284 us (0.37)
  waiting for transfers between devices: 451 us -> 99.7 us
  other arithmetic: 130 us -> 0 us
  local copies, waits for them, and re-layouts: 135 us -> 28.4 us
  Pallas kernels: 0 us -> 79.2 us
  starting transfers between devices: 6.9 us -> 73.7 us
  matrix products: 33 us -> 0 us
  between operations: 14.1 us -> 0.96 us
    all_gather x2 -> x0, waiting for transfers between devices: 265 us -> none  [the longest x1 158 us: shards(): row_spectra = lax.all_gather(spectra, 'col', axis=0, tiled=True)]
    all_to_all x1 -> x4, waiting for transfers between devices: 185 us -> 6.35 us  [shards(): lax.all_to_all(sent, 'freq', split_axis=0, concat_axis=0, tiled=True)]
    ppermute x1 -> x20, waiting for transfers between devices: 0.01 us -> 93.3 us  [the longest x4 44 us: shards(): swapped.append(lax.ppermute(block, 'row', ring(2, 1)))]
    pallas_call x0 -> x9, Pallas kernels: none -> 79.2 us  [the longest x4 38.8 us: channelize(): pl.pallas_call(channelize_kernel, grid=(blocks,), in_specs=[pl.BlockSpec(...]
    dot_general x1 -> x0, other arithmetic: 69.7 us -> none  [shards(): jnp.dot(filtered, split_table(length), preferred_element_type=jnp.float32)]
    convert_element_type x1 -> x0, other arithmetic: 43.7 us -> none  [shards(): filtered = total.astype(jnp.bfloat16).reshape(in_dev * s_dev, length)]
    reshape x3 -> x0, local copies, waits for them, and re-layouts: 40.3 us -> none  [the longest x1 26.9 us: arrange(): turned.transpose(3, 0, 2, 1).reshape(width, inputs_here, parts * frames)]
    ppermute x1 -> x20, starting transfers between devices: 1.47 us -> 37.9 us  [the longest x4 15.3 us: shards(): above.append(lax.ppermute(block, 'col', down))]
  transfers between devices with their start and end apart: 4 -> 24, of which waited for: 3 -> 12; matrix products, arithmetic and copies ran while one was open for 9% -> 0% of each run, Pallas kernels for 0% -> 19%
where the time goes in v1:
time: 284 us; the launch traced here: 282 us
  waiting for transfers between devices  99.7 us (35%)
  Pallas kernels  79.2 us (28%)
  starting transfers between devices  73.7 us (26%)
  local copies, waits for them, and re-layouts  28.4 us (10%)
    ppermute x4, waiting for transfers between devices, shards(): swapped.append(lax.ppermute(block, 'row', ring(2, 1)))  44 us
    ppermute x2, waiting for transfers between devices, shards(): across.append(lax.ppermute(above[-1], 'col', down))  42.4 us
    pallas_call x4, Pallas kernels, channelize(): pl.pallas_call(channelize_kernel, grid=(blocks,), in_specs=[pl.BlockSpec(...  38.8 us
    all_to_all x4, starting transfers between devices, shards(): lax.all_to_all(sent, 'freq', split_axis=0, concat_axis=0, tiled=True)  35.8 us
    pallas_call x1, Pallas kernels, correlate(): pl.pallas_call(functools.partial(correlate_kernel, chunks, 1.0 / depth),...  25.6 us
    unnamed x30, local copies, waits for them, and re-layouts  24.2 us
    ppermute x4, starting transfers between devices, shards(): above.append(lax.ppermute(block, 'col', down))  15.3 us
    pallas_call x4, Pallas kernels, turn(): pl.pallas_call(turn_kernel, out_shape=jax.ShapeDtypeStruct((chans, 2 * n_...  14.8 us
  transfers between devices with their start and end apart: 24, of which 12 were waited for; matrix products, arithmetic and copies ran while one was open for 0% of the time, Pallas kernels for 19%

profile of v1, /device:TPU:0, one launch (start us, length us, event | category | flops | bytes accessed | tf_op | source)
XLA Modules:
  0.0 282.0 jit_solution(11322194871207722380)
XLA Ops:
  0.6 0.0 copy-start
  0.6 4.2 %fusion = (bf16[16,16,2048]{2,1,0:T(8,128)(2,1)S(1)}, bf16[16,16,2048]{2,1,0:T(8,128)(2,1)}, bf16[16,16,2048]{2,1,0:T(8,128)(2,1)}, bf16[16,16,2048]{2,1,0:T(8,128)(2,1)}) fusion(bf16[64,16,2048]{2,1,0:T(8,128)(2,1)} %v_ref.7), kind=kLoop, calls=%fused_computation | loop fusion | bytes 8388608 | tf_op jit(solution)/shard_map/slice | solution.py:197
  4.8 1.4 collective-permute-start.3
  6.2 1.3 collective-permute-start.2
  7.5 2.0 collective-permute-done.3.h_ref
  9.5 2.2 copy-done.4
  11.7 0.9 copy-done.8
  12.6 9.7 %channelize.7 = bf16[16,16,16,128]{3,2,1,0:T(8,128)(2,1)} custom-call(bf16[64,16,2048]{2,1,0:T(8,128)(2,1)S(1)} %copy-done.4, bf16[16,16,2048]{2,1,0:T(8,128)(2,1)S(1)} %collective-permute-done.3.h_ref, f32[16,2048]{1,0:T(8,128)S(1)} %copy-done.8, bf16[8,2048,256]{2,1,0:T(8,128)(2,1)S(1)} %copy-done), custom_call_target="tpu_custom_call" | custom-call | flops 2147483648 | bytes 12582912 | tf_op jit(solution)/shard_map/channelize/pallas_call | solution.py:68
  22.3 17.5 %all-to-all-start.3 = ((bf16[16,16,16,128]{3,2,1,0:T(8,128)(2,1)}), bf16[16,16,16,128]{3,2,1,0:T(8,128)(2,1)}, u32[]{:S(2)}, u32[]{:S(2)}) async-start(bf16[16,16,16,128]{3,2,1,0:T(8,128)(2,1)} %channelize.7), calls=%async_computation.3 | async-start | bytes 2097152 | tf_op jit(solution)/shard_map/all_to_all | solution.py:199
  39.8 1.3 collective-permute-start.1
  41.1 0.0 collective-permute-done.2.h_ref
  41.2 0.0 copy-start.1
  41.2 3.4 %copy-done.1 = bf16[8,2048,256]{2,1,0:T(8,128)(2,1)S(1)} copy-done((bf16[8,2048,256]{2,1,0:T(8,128)(2,1)S(1)}, bf16[8,2048,256]{2,1,0:T(8,128)(2,1)}, u32[]{:S(2)}) %copy-start.1) | copy-done | bytes 8388632
  44.5 2.2 copy-done.5
  46.7 9.7 %channelize.6 = bf16[16,16,16,128]{3,2,1,0:T(8,128)(2,1)} custom-call(bf16[64,16,2048]{2,1,0:T(8,128)(2,1)S(1)} %copy-done.5, bf16[16,16,2048]{2,1,0:T(8,128)(2,1)S(1)} %collective-permute-done.2.h_ref, f32[16,2048]{1,0:T(8,128)S(1)} %copy-done.9, bf16[8,2048,256]{2,1,0:T(8,128)(2,1)S(1)} %copy-done.1), custom_call_target="tpu_custom_call" | custom-call | flops 2147483648 | bytes 12582912 | tf_op jit(solution)/shard_map/channelize/pallas_call | solution.py:68
  56.4 0.0 all-to-all-done.3.x_ref
  56.5 6.6 %all-to-all-start.2 = ((bf16[16,16,16,128]{3,2,1,0:T(8,128)(2,1)}), bf16[16,16,16,128]{3,2,1,0:T(8,128)(2,1)}, u32[]{:S(2)}, u32[]{:S(2)}) async-start(bf16[16,16,16,128]{3,2,1,0:T(8,128)(2,1)} %channelize.6), calls=%async_computation.2 | async-start | bytes 2097152 | tf_op jit(solution)/shard_map/all_to_all | solution.py:199
  63.1 1.3 collective-permute-start
  64.4 0.0 collective-permute-done.1.h_ref
  64.4 0.0 copy-start.2
  64.4 3.4 %copy-done.2 = bf16[8,2048,256]{2,1,0:T(8,128)(2,1)S(1)} copy-done((bf16[8,2048,256]{2,1,0:T(8,128)(2,1)S(1)}, bf16[8,2048,256]{2,1,0:T(8,128)(2,1)}, u32[]{:S(2)}) %copy-start.2) | copy-done | bytes 8388632
  67.8 2.2 copy-done.6
  70.0 9.7 %channelize.5 = bf16[16,16,16,128]{3,2,1,0:T(8,128)(2,1)} custom-call(bf16[64,16,2048]{2,1,0:T(8,128)(2,1)S(1)} %copy-done.6, bf16[16,16,2048]{2,1,0:T(8,128)(2,1)S(1)} %collective-permute-done.1.h_ref, f32[16,2048]{1,0:T(8,128)S(1)} %copy-done.9, bf16[8,2048,256]{2,1,0:T(8,128)(2,1)S(1)} %copy-done.2), custom_call_target="tpu_custom_call" | custom-call | flops 2147483648 | bytes 12582912 | tf_op jit(solution)/shard_map/channelize/pallas_call | solution.py:68
  79.7 0.1 all-to-all-done.2.x_ref
  79.7 6.6 %all-to-all-start.1 = ((bf16[16,16,16,128]{3,2,1,0:T(8,128)(2,1)}), bf16[16,16,16,128]{3,2,1,0:T(8,128)(2,1)}, u32[]{:S(2)}, u32[]{:S(2)}) async-start(bf16[16,16,16,128]{3,2,1,0:T(8,128)(2,1)} %channelize.5), calls=%async_computation.1 | async-start | bytes 2097152 | tf_op jit(solution)/shard_map/all_to_all | solution.py:199
  86.3 3.2 %turn.7.refs_3_ = bf16[64,32,256]{2,1,0:T(8,128)(2,1)S(1)} custom-call(bf16[16,16,16,128]{3,2,1,0:T(8,128)(2,1)} %all-to-all-done.3.x_ref), custom_call_target="tpu_custom_call" | custom-call | flops 1000000000 | bytes 4194304 | tf_op jit(solution)/shard_map/turn/pallas_call | solution.py:111
  89.5 2.8 %collective-permute-start.19 = (bf16[64,32,256]{2,1,0:T(8,128)(2,1)S(1)}, bf16[64,32,256]{2,1,0:T(8,128)(2,1)}, u32[]{:S(2)}, u32[]{:S(2)}) collective-permute-start(bf16[64,32,256]{2,1,0:T(8,128)(2,1)S(1)} %turn.7.refs_3_), channel_id=1, source_target_pairs={{0,4},{4,0},{1,5},{5,1},{2,6},{6,2},{3,7},{7,3},{8,12},{12,8},{9,1... | collective-permute-start | bytes 3145736 | tf_op jit(solution)/shard_map/ppermute | solution.py:208
  92.4 3.4 %copy-done.3 = bf16[8,2048,256]{2,1,0:T(8,128)(2,1)S(1)} copy-done((bf16[8,2048,256]{2,1,0:T(8,128)(2,1)S(1)}, bf16[8,2048,256]{2,1,0:T(8,128)(2,1)}, u32[]{:S(2)}) %copy-start.3) | copy-done | bytes 8388632
  95.7 2.2 copy-done.7
  97.9 9.7 %channelize.4 = bf16[16,16,16,128]{3,2,1,0:T(8,128)(2,1)} custom-call(bf16[64,16,2048]{2,1,0:T(8,128)(2,1)S(1)} %copy-done.7, bf16[16,16,2048]{2,1,0:T(8,128)(2,1)S(1)} %collective-permute-done.h_ref, f32[16,2048]{1,0:T(8,128)S(1)} %copy-done.9, bf16[8,2048,256]{2,1,0:T(8,128)(2,1)S(1)} %copy-done.3), custom_call_target="tpu_custom_call" | custom-call | flops 2147483648 | bytes 12582912 | tf_op jit(solution)/shard_map/channelize/pallas_call | solution.py:68
  107.6 4.0 %collective-permute-start.11 = (bf16[64,32,256]{2,1,0:T(8,128)(2,1)S(1)}, bf16[64,32,256]{2,1,0:T(8,128)(2,1)S(1)}, u32[]{:S(2)}, u32[]{:S(2)}) collective-permute-start(bf16[64,32,256]{2,1,0:T(8,128)(2,1)S(1)} %turn.7.refs_3_), channel_id=1, source_target_pairs={{0,3},{1,0},{2,1},{3,2},{4,7},{5,4},{6,5},{7,6},{8,11},{9,8},{10,9... | collective-permute-start | bytes 3145736 | tf_op jit(solution)/shard_map/ppermute | solution.py:203
  111.7 5.1 %all-to-all-start = ((bf16[16,16,16,128]{3,2,1,0:T(8,128)(2,1)}), bf16[16,16,16,128]{3,2,1,0:T(8,128)(2,1)}, u32[]{:S(2)}, u32[]{:S(2)}) async-start(bf16[16,16,16,128]{3,2,1,0:T(8,128)(2,1)} %channelize.4), calls=%async_computation | async-start | bytes 2097152 | tf_op jit(solution)/shard_map/all_to_all | solution.py:199
  116.8 4.2 %turn.6.refs_2_ = bf16[64,32,256]{2,1,0:T(8,128)(2,1)} custom-call(bf16[16,16,16,128]{3,2,1,0:T(8,128)(2,1)} %all-to-all-done.2.x_ref), custom_call_target="tpu_custom_call" | custom-call | flops 1000000000 | bytes 4194304 | tf_op jit(solution)/shard_map/turn/pallas_call | solution.py:111
  121.0 2.0 collective-permute-start.18
  123.0 3.2 %collective-permute-start.10 = (bf16[64,32,256]{2,1,0:T(8,128)(2,1)}, bf16[64,32,256]{2,1,0:T(8,128)(2,1)}, u32[]{:S(2)}, u32[]{:S(2)}) collective-permute-start(bf16[64,32,256]{2,1,0:T(8,128)(2,1)} %turn.6.refs_2_), channel_id=1, source_target_pairs={{0,3},{1,0},{2,1},{3,2},{4,7},{5,4},{6,5},{7,6},{8,11},{9,8},{10,9... | collective-permute-start | bytes 3145736 | tf_op jit(solution)/shard_map/ppermute | solution.py:203
  126.2 0.6 collective-permute-start.6
  126.8 3.2 %turn.5.refs_1_ = bf16[64,32,256]{2,1,0:T(8,128)(2,1)S(1)} custom-call(bf16[16,16,16,128]{3,2,1,0:T(8,128)(2,1)} %all-to-all-done.1.x_ref), custom_call_target="tpu_custom_call" | custom-call | flops 1000000000 | bytes 4194304 | tf_op jit(solution)/shard_map/turn/pallas_call | solution.py:111
  130.0 0.0 copy-start.10
  130.0 1.0 copy-done.10
  131.0 6.2 %all-to-all-done.x_ref = bf16[16,16,16,128]{3,2,1,0:T(8,128)(2,1)} async-done(((bf16[16,16,16,128]{3,2,1,0:T(8,128)(2,1)}), bf16[16,16,16,128]{3,2,1,0:T(8,128)(2,1)}, u32[]{:S(2)}, u32[]{:S(2)}) %all-to-all-start) | async-done | bytes 1048608 | tf_op jit(solution)/shard_map/all_to_all | solution.py:199
  137.2 4.2 %turn.4.refs_0_ = bf16[64,32,256]{2,1,0:T(8,128)(2,1)} custom-call(bf16[16,16,16,128]{3,2,1,0:T(8,128)(2,1)} %all-to-all-done.x_ref), custom_call_target="tpu_custom_call" | custom-call | flops 1000000000 | bytes 4194304 | tf_op jit(solution)/shard_map/turn/pallas_call | solution.py:111
  141.4 2.7 collective-permute-start.17
  144.2 4.0 %collective-permute-start.9 = (bf16[64,32,256]{2,1,0:T(8,128)(2,1)}, bf16[64,32,256]{2,1,0:T(8,128)(2,1)}, u32[]{:S(2)}, u32[]{:S(2)}) collective-permute-start(bf16[64,32,256]{2,1,0:T(8,128)(2,1)} %copy-done.10), channel_id=1, source_target_pairs={{0,3},{1,0},{2,1},{3,2},{4,7},{5,4},{6,5},{7,6},{8,11},{9,8},{10,9... | collective-permute-start | bytes 3145736 | tf_op jit(solution)/shard_map/ppermute | solution.py:203
  148.2 10.8 %collective-permute-done.18.refs_18_ = bf16[64,32,256]{2,1,0:T(8,128)(2,1)} collective-permute-done((bf16[64,32,256]{2,1,0:T(8,128)(2,1)}, bf16[64,32,256]{2,1,0:T(8,128)(2,1)}, u32[]{:S(2)}, u32[]{:S(2)}) %collective-permute-start.18) | collective-permute-done | bytes 1048608 | tf_op jit(solution)/shard_map/ppermute | solution.py:208
  158.9 1.9 collective-permute-start.5
  160.8 0.8 collective-permute-start.16
  161.6 1.9 collective-permute-start.4
  163.5 17.8 %collective-permute-done.17.refs_17_ = bf16[64,32,256]{2,1,0:T(8,128)(2,1)S(1)} collective-permute-done((bf16[64,32,256]{2,1,0:T(8,128)(2,1)}, bf16[64,32,256]{2,1,0:T(8,128)(2,1)S(1)}, u32[]{:S(2)}, u32[]{:S(2)}) %collective-permute-start.17) | collective-permute-done | bytes 1048608 | tf_op jit(solution)/shard_map/ppermute | solution.py:208
  181.3 4.0 %collective-permute-start.8 = (bf16[64,32,256]{2,1,0:T(8,128)(2,1)}, bf16[64,32,256]{2,1,0:T(8,128)(2,1)}, u32[]{:S(2)}, u32[]{:S(2)}) collective-permute-start(bf16[64,32,256]{2,1,0:T(8,128)(2,1)} %turn.4.refs_0_), channel_id=1, source_target_pairs={{0,3},{1,0},{2,1},{3,2},{4,7},{5,4},{6,5},{7,6},{8,11},{9,8},{10,9... | collective-permute-start | bytes 3145736 | tf_op jit(solution)/shard_map/ppermute | solution.py:203
  185.3 0.4 collective-permute-start.15
  185.7 1.4 collective-permute-done.5.refs_5_
  187.2 1.0 copy-done.12
  188.1 0.2 collective-permute-start.14
  188.3 15.4 %collective-permute-done.16.refs_16_ = bf16[64,32,256]{2,1,0:T(8,128)(2,1)} collective-permute-done((bf16[64,32,256]{2,1,0:T(8,128)(2,1)}, bf16[64,32,256]{2,1,0:T(8,128)(2,1)}, u32[]{:S(2)}, u32[]{:S(2)}) %collective-permute-start.16) | collective-permute-done | bytes 1048608 | tf_op jit(solution)/shard_map/ppermute | solution.py:208
  203.7 4.0 %collective-permute-start.13 = (bf16[64,32,256]{2,1,0:T(8,128)(2,1)}, bf16[64,32,256]{2,1,0:T(8,128)(2,1)}, u32[]{:S(2)}, u32[]{:S(2)}) collective-permute-start(bf16[64,32,256]{2,1,0:T(8,128)(2,1)} %collective-permute-done.9.refs_9_), channel_id=1, source_target_pairs={{0,3},{1,0},{2,1},{3,2},{4,7},{5,4},{6,5},{7,6},{8,11},{9,8},{10,9... | collective-permute-start | bytes 3145736 | tf_op jit(solution)/shard_map/ppermute | solution.py:207
  207.7 2.0 collective-permute-done.4.refs_4_
  209.7 0.1 stack.23.place
  209.8 21.8 %collective-permute-done.15.refs_15_ = bf16[64,32,256]{2,1,0:T(8,128)(2,1)} collective-permute-done((bf16[64,32,256]{2,1,0:T(8,128)(2,1)S(1)}, bf16[64,32,256]{2,1,0:T(8,128)(2,1)}, u32[]{:S(2)}, u32[]{:S(2)}) %collective-permute-start.15) | collective-permute-done | bytes 1048608 | tf_op jit(solution)/shard_map/ppermute | solution.py:207
  231.6 0.6 collective-permute-done.14.refs_14_
  232.2 20.7 %collective-permute-done.13.refs_13_ = bf16[64,32,256]{2,1,0:T(8,128)(2,1)} collective-permute-done((bf16[64,32,256]{2,1,0:T(8,128)(2,1)}, bf16[64,32,256]{2,1,0:T(8,128)(2,1)}, u32[]{:S(2)}, u32[]{:S(2)}) %collective-permute-start.13) | collective-permute-done | bytes 1048608 | tf_op jit(solution)/shard_map/ppermute | solution.py:207
  252.9 0.8 collective-permute-done.12.refs_12_
  253.7 1.2 copy-done.11
  255.0 1.2 copy-done.13
  256.2 25.6 %correlate.1 = (f32[64,256,128]{2,1,0:T(8,128)}, f32[64,256,128]{2,1,0:T(8,128)}) custom-call(s32[5]{0:T(128)S(1)} %stack.23.place, bf16[64,32,256]{2,1,0:T(8,128)(2,1)} %turn.4.refs_0_, bf16[64,32,256]{2,1,0:T(8,128)(2,1)S(1)} %copy-done.11, bf16[64,32,256]{2,1,0:T(8,128)(2,1)} %turn.6.refs_2_, bf16[64,32,256]{2,1,0:T(8,128)(2,1)S(1)} %turn.7.refs_3_, ...), custom_call_target="tpu_custom_call" | custom-call | flops 4294967296 | bytes 37748736 | tf_op jit(solution)/shard_map/correlate/pallas_call | solution.py:164
  (25 shorter events, 0.1 us)
Async XLA Ops:
  0.6 8.9 %copy-start = (bf16[8,2048,256]{2,1,0:T(8,128)(2,1)S(1)}, bf16[8,2048,256]{2,1,0:T(8,128)(2,1)}, u32[]{:S(2)}) copy-start(bf16[8,2048,256]{2,1,0:T(8,128)(2,1)} %constant.37.clone.t_ref) | copy-start | bytes 25165828
  4.8 4.7 %collective-permute-start.3 = (bf16[16,16,2048]{2,1,0:T(8,128)(2,1)S(1)}, bf16[16,16,2048]{2,1,0:T(8,128)(2,1)S(1)}, u32[]{:S(2)}, u32[]{:S(2)}) collective-permute-start(bf16[16,16,2048]{2,1,0:T(8,128)(2,1)S(1)} %get-tuple-element.2), channel_id=1, source_target_pairs={{8,0},{16,8},{24,16},{32,24},{40,32},{48,40},{56,48},{64,56},{72,6... | collective-permute-start | bytes 3145736 | tf_op jit(solution)/shard_map/ppermute | solution.py:197
  6.2 34.9 %collective-permute-start.2 = (bf16[16,16,2048]{2,1,0:T(8,128)(2,1)}, bf16[16,16,2048]{2,1,0:T(8,128)(2,1)S(1)}, u32[]{:S(2)}, u32[]{:S(2)}) collective-permute-start(bf16[16,16,2048]{2,1,0:T(8,128)(2,1)} %get-tuple-element.3), channel_id=1, source_target_pairs={{8,0},{16,8},{24,16},{32,24},{40,32},{48,40},{56,48},{64,56},{72,6... | collective-permute-start | bytes 3145736 | tf_op jit(solution)/shard_map/ppermute | solution.py:197
  9.5 2.2 copy-start.4
  11.7 0.9 copy-start.8
  12.6 28.6 %copy-start.9 = (f32[16,2048]{1,0:T(8,128)S(1)}, f32[16,2048]{1,0:T(8,128)}, u32[]{:S(2)}) copy-start(f32[16,2048]{1,0:T(8,128)} %w_ref.7) | copy-start | bytes 393220
  22.3 34.2 %all-to-all-start.3 = ((bf16[16,16,16,128]{3,2,1,0:T(8,128)(2,1)}), bf16[16,16,16,128]{3,2,1,0:T(8,128)(2,1)}, u32[]{:S(2)}, u32[]{:S(2)}) async-start(bf16[16,16,16,128]{3,2,1,0:T(8,128)(2,1)} %channelize.7), calls=%async_computation.3 | async-start | bytes 2097152 | tf_op jit(solution)/shard_map/all_to_all | solution.py:199
  39.8 24.6 %collective-permute-start.1 = (bf16[16,16,2048]{2,1,0:T(8,128)(2,1)}, bf16[16,16,2048]{2,1,0:T(8,128)(2,1)S(1)}, u32[]{:S(2)}, u32[]{:S(2)}) collective-permute-start(bf16[16,16,2048]{2,1,0:T(8,128)(2,1)} %get-tuple-element.4), channel_id=1, source_target_pairs={{8,0},{16,8},{24,16},{32,24},{40,32},{48,40},{56,48},{64,56},{72,6... | collective-permute-start | bytes 3145736 | tf_op jit(solution)/shard_map/ppermute | solution.py:197
  41.2 3.4 %copy-start.1 = (bf16[8,2048,256]{2,1,0:T(8,128)(2,1)S(1)}, bf16[8,2048,256]{2,1,0:T(8,128)(2,1)}, u32[]{:S(2)}) copy-start(bf16[8,2048,256]{2,1,0:T(8,128)(2,1)} %constant.37.clone.t_ref) | copy-start | bytes 25165828
  44.5 2.2 copy-start.5
  56.5 23.3 %all-to-all-start.2 = ((bf16[16,16,16,128]{3,2,1,0:T(8,128)(2,1)}), bf16[16,16,16,128]{3,2,1,0:T(8,128)(2,1)}, u32[]{:S(2)}, u32[]{:S(2)}) async-start(bf16[16,16,16,128]{3,2,1,0:T(8,128)(2,1)} %channelize.6), calls=%async_computation.2 | async-start | bytes 2097152 | tf_op jit(solution)/shard_map/all_to_all | solution.py:199
  63.1 29.3 %collective-permute-start = (bf16[16,16,2048]{2,1,0:T(8,128)(2,1)}, bf16[16,16,2048]{2,1,0:T(8,128)(2,1)S(1)}, u32[]{:S(2)}, u32[]{:S(2)}) collective-permute-start(bf16[16,16,2048]{2,1,0:T(8,128)(2,1)} %get-tuple-element.5), channel_id=1, source_target_pairs={{8,0},{16,8},{24,16},{32,24},{40,32},{48,40},{56,48},{64,56},{72,6... | collective-permute-start | bytes 3145736 | tf_op jit(solution)/shard_map/ppermute | solution.py:197
  64.4 3.4 %copy-start.2 = (bf16[8,2048,256]{2,1,0:T(8,128)(2,1)S(1)}, bf16[8,2048,256]{2,1,0:T(8,128)(2,1)}, u32[]{:S(2)}) copy-start(bf16[8,2048,256]{2,1,0:T(8,128)(2,1)} %constant.37.clone.t_ref) | copy-start | bytes 25165828
  67.8 2.2 copy-start.6
  79.7 31.9 %all-to-all-start.1 = ((bf16[16,16,16,128]{3,2,1,0:T(8,128)(2,1)}), bf16[16,16,16,128]{3,2,1,0:T(8,128)(2,1)}, u32[]{:S(2)}, u32[]{:S(2)}) async-start(bf16[16,16,16,128]{3,2,1,0:T(8,128)(2,1)} %channelize.5), calls=%async_computation.1 | async-start | bytes 2097152 | tf_op jit(solution)/shard_map/all_to_all | solution.py:199
  89.5 36.7 %collective-permute-start.19 = (bf16[64,32,256]{2,1,0:T(8,128)(2,1)S(1)}, bf16[64,32,256]{2,1,0:T(8,128)(2,1)}, u32[]{:S(2)}, u32[]{:S(2)}) collective-permute-start(bf16[64,32,256]{2,1,0:T(8,128)(2,1)S(1)} %turn.7.refs_3_), channel_id=1, source_target_pairs={{0,4},{4,0},{1,5},{5,1},{2,6},{6,2},{3,7},{7,3},{8,12},{12,8},{9,1... | collective-permute-start | bytes 3145736 | tf_op jit(solution)/shard_map/ppermute | solution.py:208
  92.3 3.4 %copy-start.3 = (bf16[8,2048,256]{2,1,0:T(8,128)(2,1)S(1)}, bf16[8,2048,256]{2,1,0:T(8,128)(2,1)}, u32[]{:S(2)}) copy-start(bf16[8,2048,256]{2,1,0:T(8,128)(2,1)} %constant.37.clone.t_ref) | copy-start | bytes 25165828
  95.7 2.2 copy-start.7
  107.6 33.8 %collective-permute-start.11 = (bf16[64,32,256]{2,1,0:T(8,128)(2,1)S(1)}, bf16[64,32,256]{2,1,0:T(8,128)(2,1)S(1)}, u32[]{:S(2)}, u32[]{:S(2)}) collective-permute-start(bf16[64,32,256]{2,1,0:T(8,128)(2,1)S(1)} %turn.7.refs_3_), channel_id=1, source_target_pairs={{0,3},{1,0},{2,1},{3,2},{4,7},{5,4},{6,5},{7,6},{8,11},{9,8},{10,9... | collective-permute-start | bytes 3145736 | tf_op jit(solution)/shard_map/ppermute | solution.py:203
  111.7 32.5 %collective-permute-start.7 = (bf16[64,32,256]{2,1,0:T(8,128)(2,1)S(1)}, bf16[64,32,256]{2,1,0:T(8,128)(2,1)S(1)}, u32[]{:S(2)}, u32[]{:S(2)}) collective-permute-start(bf16[64,32,256]{2,1,0:T(8,128)(2,1)S(1)} %turn.7.refs_3_), channel_id=1, source_target_pairs={{0,1},{1,2},{2,3},{3,0},{4,5},{5,6},{6,7},{7,4},{8,9},{9,10},{10,1... | collective-permute-start | bytes 3145736 | tf_op jit(solution)/shard_map/ppermute | solution.py:202
  111.7 25.5 %all-to-all-start = ((bf16[16,16,16,128]{3,2,1,0:T(8,128)(2,1)}), bf16[16,16,16,128]{3,2,1,0:T(8,128)(2,1)}, u32[]{:S(2)}, u32[]{:S(2)}) async-start(bf16[16,16,16,128]{3,2,1,0:T(8,128)(2,1)} %channelize.4), calls=%async_computation | async-start | bytes 2097152 | tf_op jit(solution)/shard_map/all_to_all | solution.py:199
  121.0 38.0 %collective-permute-start.18 = (bf16[64,32,256]{2,1,0:T(8,128)(2,1)}, bf16[64,32,256]{2,1,0:T(8,128)(2,1)}, u32[]{:S(2)}, u32[]{:S(2)}) collective-permute-start(bf16[64,32,256]{2,1,0:T(8,128)(2,1)} %turn.6.refs_2_), channel_id=1, source_target_pairs={{0,4},{4,0},{1,5},{5,1},{2,6},{6,2},{3,7},{7,3},{8,12},{12,8},{9,1... | collective-permute-start | bytes 3145736 | tf_op jit(solution)/shard_map/ppermute | solution.py:208
  123.0 37.8 %collective-permute-start.10 = (bf16[64,32,256]{2,1,0:T(8,128)(2,1)}, bf16[64,32,256]{2,1,0:T(8,128)(2,1)}, u32[]{:S(2)}, u32[]{:S(2)}) collective-permute-start(bf16[64,32,256]{2,1,0:T(8,128)(2,1)} %turn.6.refs_2_), channel_id=1, source_target_pairs={{0,3},{1,0},{2,1},{3,2},{4,7},{5,4},{6,5},{7,6},{8,11},{9,8},{10,9... | collective-permute-start | bytes 3145736 | tf_op jit(solution)/shard_map/ppermute | solution.py:203
  126.2 35.4 %collective-permute-start.6 = (bf16[64,32,256]{2,1,0:T(8,128)(2,1)}, bf16[64,32,256]{2,1,0:T(8,128)(2,1)}, u32[]{:S(2)}, u32[]{:S(2)}) collective-permute-start(bf16[64,32,256]{2,1,0:T(8,128)(2,1)} %turn.6.refs_2_), channel_id=1, source_target_pairs={{0,1},{1,2},{2,3},{3,0},{4,5},{5,6},{6,7},{7,4},{8,9},{9,10},{10,1... | collective-permute-start | bytes 3145736 | tf_op jit(solution)/shard_map/ppermute | solution.py:202
  130.0 1.0 copy-start.10
  141.4 39.9 %collective-permute-start.17 = (bf16[64,32,256]{2,1,0:T(8,128)(2,1)}, bf16[64,32,256]{2,1,0:T(8,128)(2,1)S(1)}, u32[]{:S(2)}, u32[]{:S(2)}) collective-permute-start(bf16[64,32,256]{2,1,0:T(8,128)(2,1)} %copy-done.10), channel_id=1, source_target_pairs={{0,4},{4,0},{1,5},{5,1},{2,6},{6,2},{3,7},{7,3},{8,12},{12,8},{9,1... | collective-permute-start | bytes 3145736 | tf_op jit(solution)/shard_map/ppermute | solution.py:208
  144.2 41.2 %collective-permute-start.9 = (bf16[64,32,256]{2,1,0:T(8,128)(2,1)}, bf16[64,32,256]{2,1,0:T(8,128)(2,1)}, u32[]{:S(2)}, u32[]{:S(2)}) collective-permute-start(bf16[64,32,256]{2,1,0:T(8,128)(2,1)} %copy-done.10), channel_id=1, source_target_pairs={{0,3},{1,0},{2,1},{3,2},{4,7},{5,4},{6,5},{7,6},{8,11},{9,8},{10,9... | collective-permute-start | bytes 3145736 | tf_op jit(solution)/shard_map/ppermute | solution.py:203
  158.9 28.2 %collective-permute-start.5 = (bf16[64,32,256]{2,1,0:T(8,128)(2,1)}, bf16[64,32,256]{2,1,0:T(8,128)(2,1)S(1)}, u32[]{:S(2)}, u32[]{:S(2)}) collective-permute-start(bf16[64,32,256]{2,1,0:T(8,128)(2,1)} %copy-done.10), channel_id=1, source_target_pairs={{0,1},{1,2},{2,3},{3,0},{4,5},{5,6},{6,7},{7,4},{8,9},{9,10},{10,1... | collective-permute-start | bytes 3145736 | tf_op jit(solution)/shard_map/ppermute | solution.py:202
  160.8 42.9 %collective-permute-start.16 = (bf16[64,32,256]{2,1,0:T(8,128)(2,1)}, bf16[64,32,256]{2,1,0:T(8,128)(2,1)}, u32[]{:S(2)}, u32[]{:S(2)}) collective-permute-start(bf16[64,32,256]{2,1,0:T(8,128)(2,1)} %turn.4.refs_0_), channel_id=1, source_target_pairs={{0,4},{4,0},{1,5},{5,1},{2,6},{6,2},{3,7},{7,3},{8,12},{12,8},{9,1... | collective-permute-start | bytes 3145736 | tf_op jit(solution)/shard_map/ppermute | solution.py:208
  161.6 48.1 %collective-permute-start.4 = (bf16[64,32,256]{2,1,0:T(8,128)(2,1)}, bf16[64,32,256]{2,1,0:T(8,128)(2,1)}, u32[]{:S(2)}, u32[]{:S(2)}) collective-permute-start(bf16[64,32,256]{2,1,0:T(8,128)(2,1)} %turn.4.refs_0_), channel_id=1, source_target_pairs={{0,1},{1,2},{2,3},{3,0},{4,5},{5,6},{6,7},{7,4},{8,9},{9,10},{10,1... | collective-permute-start | bytes 3145736 | tf_op jit(solution)/shard_map/ppermute | solution.py:202
  181.3 5.8 %copy-start.14 = (bf16[64,32,256]{2,1,0:T(8,128)(2,1)}, bf16[64,32,256]{2,1,0:T(8,128)(2,1)S(1)}, u32[]{:S(2)}) copy-start(bf16[64,32,256]{2,1,0:T(8,128)(2,1)S(1)} %collective-permute-done.17.refs_17_) | copy-start | bytes 3145732
  181.3 28.5 %collective-permute-start.8 = (bf16[64,32,256]{2,1,0:T(8,128)(2,1)}, bf16[64,32,256]{2,1,0:T(8,128)(2,1)}, u32[]{:S(2)}, u32[]{:S(2)}) collective-permute-start(bf16[64,32,256]{2,1,0:T(8,128)(2,1)} %turn.4.refs_0_), channel_id=1, source_target_pairs={{0,3},{1,0},{2,1},{3,2},{4,7},{5,4},{6,5},{7,6},{8,11},{9,8},{10,9... | collective-permute-start | bytes 3145736 | tf_op jit(solution)/shard_map/ppermute | solution.py:203
  185.3 46.3 %collective-permute-start.15 = (bf16[64,32,256]{2,1,0:T(8,128)(2,1)S(1)}, bf16[64,32,256]{2,1,0:T(8,128)(2,1)}, u32[]{:S(2)}, u32[]{:S(2)}) collective-permute-start(bf16[64,32,256]{2,1,0:T(8,128)(2,1)S(1)} %collective-permute-done.11.refs_11_), channel_id=1, source_target_pairs={{0,3},{1,0},{2,1},{3,2},{4,7},{5,4},{6,5},{7,6},{8,11},{9,8},{10,9... | collective-permute-start | bytes 3145736 | tf_op jit(solution)/shard_map/ppermute | solution.py:207
  187.1 1.0 copy-start.12
  188.1 44.1 %collective-permute-start.14 = (bf16[64,32,256]{2,1,0:T(8,128)(2,1)}, bf16[64,32,256]{2,1,0:T(8,128)(2,1)}, u32[]{:S(2)}, u32[]{:S(2)}) collective-permute-start(bf16[64,32,256]{2,1,0:T(8,128)(2,1)} %collective-permute-done.6.refs_6_), channel_id=1, source_target_pairs={{0,1},{1,2},{2,3},{3,0},{4,5},{5,6},{6,7},{7,4},{8,9},{9,10},{10,1... | collective-permute-start | bytes 3145736 | tf_op jit(solution)/shard_map/ppermute | solution.py:205
  203.7 49.2 %collective-permute-start.13 = (bf16[64,32,256]{2,1,0:T(8,128)(2,1)}, bf16[64,32,256]{2,1,0:T(8,128)(2,1)}, u32[]{:S(2)}, u32[]{:S(2)}) collective-permute-start(bf16[64,32,256]{2,1,0:T(8,128)(2,1)} %collective-permute-done.9.refs_9_), channel_id=1, source_target_pairs={{0,3},{1,0},{2,1},{3,2},{4,7},{5,4},{6,5},{7,6},{8,11},{9,8},{10,9... | collective-permute-start | bytes 3145736 | tf_op jit(solution)/shard_map/ppermute | solution.py:207
  209.7 44.0 %collective-permute-start.12 = (bf16[64,32,256]{2,1,0:T(8,128)(2,1)}, bf16[64,32,256]{2,1,0:T(8,128)(2,1)}, u32[]{:S(2)}, u32[]{:S(2)}) collective-permute-start(bf16[64,32,256]{2,1,0:T(8,128)(2,1)} %collective-permute-done.4.refs_4_), channel_id=1, source_target_pairs={{0,1},{1,2},{2,3},{3,0},{4,5},{5,6},{6,7},{7,4},{8,9},{9,10},{10,1... | collective-permute-start | bytes 3145736 | tf_op jit(solution)/shard_map/ppermute | solution.py:205
  253.7 1.2 copy-start.11
  255.0 1.2 copy-start.13

commit v2 on v1

v2 whole, which is shorter than its diff:
```python
import functools
import math

import jax
import jax.numpy as jnp
import ml_dtypes
import numpy as np
from jax import lax
from jax.experimental import pallas as pl
from jax.experimental.pallas import tpu as pltpu
from jax.sharding import PartitionSpec as P

LANES = 128
CHUNKS = 4
COLS = 512
PARTS = 2
SHORT = pl.CostEstimate(flops=10**8, bytes_accessed=2**17, transcendentals=0)
VMEM = 56 * 2**20


def dft_table(length, groups):
    half = length // 2
    base = np.arange(length) * (2.0 * math.pi / length)
    cosine = np.cos(base) / math.sqrt(length)
    sine = -np.sin(base) / math.sqrt(length)
    phase = np.arange(length)[:, None] * np.arange(half)[None, :] % length
    parts = np.stack([cosine[phase], sine[phase]], axis=1)
    parts = parts.reshape(length, 2, groups, half // groups).transpose(0, 2, 1, 3)
    blocks = parts.reshape(length, length // COLS, COLS).transpose(1, 0, 2)
    return blocks.astype(ml_dtypes.bfloat16)


def channelize_kernel(v_ref, h_ref, w_ref, t_ref, *refs):
    u_ref, ext, acc, filt = refs[-4:]
    n_in, frames, length = v_ref.shape
    taps = w_ref.shape[0]
    depth = 2 * frames

    @pl.when(pl.program_id(0) == 0)
    def _():
        def one_tile(t, carry):
            lanes = pl.ds(pl.multiple_of(t * LANES, LANES), LANES)
            for i in range(n_in):
                ext[pl.ds(i * depth, frames), :] = v_ref[i, :, lanes].astype(jnp.float32)
                ext[pl.ds(i * depth + frames, frames), :] = h_ref[i, :, lanes].astype(jnp.float32)
            weights = [jnp.broadcast_to(w_ref[pl.ds(k, 1), lanes], (8, LANES)) for k in range(taps)]
            for i in range(n_in):
                for s in range(0, frames, 8):
                    at = i * depth + s
                    total = weights[0] * ext[pl.ds(at, 8), :]
                    for k in range(1, taps):
                        total = total + weights[k] * ext[pl.ds(at + k, 8), :]
                    acc[pl.ds(i * frames + s, 8), :] = total
            filt[:, lanes] = acc[...].astype(jnp.bfloat16)
            return carry

        lax.fori_loop(0, length // LANES, one_tile, 0)

    out = jnp.dot(filt[...], t_ref[0], preferred_element_type=jnp.float32)
    out = out.astype(jnp.bfloat16)
    for j in range(u_ref.shape[0]):
        u_ref[j] = out[:, j * LANES : (j + 1) * LANES].reshape(n_in, frames, LANES)


def channelize(chunk, n_in, voltages, halo, window, table, earlier):
    frames, length = voltages.shape[1:]
    blocks = table.shape[0]
    rows = n_in * frames
    return pl.pallas_call(
        channelize_kernel,
        grid=(blocks,),
        in_specs=[
            pl.BlockSpec((n_in, frames, length), lambda b: (chunk, 0, 0)),
            pl.BlockSpec((n_in, frames, length), lambda b: (0, 0, 0)),
            pl.BlockSpec(window.shape, lambda b: (0, 0)),
            pl.BlockSpec((1, length, COLS), lambda b: (b, 0, 0)),
            *[pl.BlockSpec(memory_space=pl.ANY)] * len(earlier),
        ],
        out_specs=pl.BlockSpec((COLS // LANES, n_in, frames, LANES), lambda b: (b, 0, 0, 0)),
        out_shape=jax.ShapeDtypeStruct((length // LANES, n_in, frames, LANES), jnp.bfloat16),
        scratch_shapes=[
            pltpu.VMEM((2 * rows, LANES), jnp.float32),
            pltpu.VMEM((rows, LANES), jnp.float32),
            pltpu.VMEM((rows, length), jnp.bfloat16),
        ],
        compiler_params=pltpu.CompilerParams(vmem_limit_bytes=VMEM),
        cost_estimate=SHORT,
        name="channelize",
    )(voltages, halo, window, table, *earlier)


def turn_kernel(parts, x_ref, *refs):
    g_refs, scr = refs[-1 - parts : -1], refs[-1]
    devices, n_in, frames, lanes = x_ref.shape
    chans = lanes // 2
    depth = devices * frames
    part = chans // len(g_refs)
    for i in range(n_in):
        block = x_ref[:, i, :, :].reshape(depth, lanes).astype(jnp.float32)
        for h in range(depth // LANES):
            piece = block[h * LANES : (h + 1) * LANES, :].T
            scr[h, pl.ds(i, chans, stride=2 * n_in), :] = piece[:chans]
            scr[h, pl.ds(n_in + i, chans, stride=2 * n_in), :] = piece[chans:]
    for h in range(depth // LANES):
        for j, g_ref in enumerate(g_refs):
            rows = scr[h, j * part * 2 * n_in : (j + 1) * part * 2 * n_in, :]
            g_ref[:, :, h * LANES : (h + 1) * LANES] = rows.reshape(part, 2 * n_in, LANES).astype(jnp.bfloat16)


def turn(received, earlier, parts):
    devices, n_in, frames, lanes = received.shape
    chans, depth = lanes // 2, devices * frames
    shape = jax.ShapeDtypeStruct((chans // parts, 2 * n_in, depth), jnp.bfloat16)
    vmem = pl.BlockSpec(memory_space=pltpu.VMEM)
    return pl.pallas_call(
        functools.partial(turn_kernel, parts),
        in_specs=[vmem] + [pl.BlockSpec(memory_space=pl.ANY)] * len(earlier),
        out_specs=[vmem] * parts,
        out_shape=[shape] * parts,
        scratch_shapes=[pltpu.VMEM((depth // LANES, chans * 2 * n_in, LANES), jnp.float32)],
        compiler_params=pltpu.CompilerParams(vmem_limit_bytes=VMEM),
        cost_estimate=SHORT,
        name="turn",
    )(received, *earlier)


def correlate_kernel(chunks, scale, place, *refs):
    blocks = refs[: 4 * chunks]
    swapped = refs[4 * chunks : 5 * chunks]
    re_ref, im_ref = refs[-2:]
    chans, twice, depth = blocks[0].shape
    n_in = twice // 2
    inputs = n_in * chunks
    half = 2 * inputs
    low = place[0] == 0
    for ch in range(chans):
        near = [ref[ch] for ref in blocks[:chunks]]
        far = [ref[ch] for ref in swapped]
        partner = []
        for part in (slice(0, n_in), slice(n_in, twice)):
            partner += [jnp.where(low, x[part], y[part]) for x, y in zip(near, far)]
            partner += [jnp.where(low, y[part], x[part]) for x, y in zip(near, far)]
        partner = jnp.concatenate(partner, axis=0)
        first = jnp.concatenate([ref[ch] for ref in blocks], axis=0)
        products = lax.dot_general(
            first, partner, (((1,), (1,)), ((), ())), preferred_element_type=jnp.float32
        )
        for d in range(4):
            at = pl.multiple_of(place[1 + d] * inputs, inputs)
            for q in range(chunks):
                start = (d * chunks + q) * twice
                re = products[start : start + n_in]
                im = products[start + n_in : start + twice]
                rows = pl.ds(at + q * n_in, n_in)
                re_ref[ch, rows, :] = (re[:, :half] + im[:, half:]) * scale
                im_ref[ch, rows, :] = (im[:, :half] - re[:, half:]) * scale


def correlate(place, blocks, swapped, part, parts, before, step=8):
    chunks = len(swapped)
    chans = max(x.shape[0] for x in swapped)
    twice, depth = swapped[0].shape[1:]
    inputs = twice // 2 * chunks
    steps = chans // parts // step
    start = part * steps
    whole = pl.BlockSpec((step, twice, depth), lambda b, place: (b + start, 0, 0))
    own = pl.BlockSpec((step, twice, depth), lambda b, place: (b, 0, 0))
    out = pl.BlockSpec((step, 4 * inputs, 2 * inputs), lambda b, place: (b + start, 0, 0))
    shape = jax.ShapeDtypeStruct((chans, 4 * inputs, 2 * inputs), jnp.float32)
    arrays = [*blocks, *swapped]
    return pl.pallas_call(
        functools.partial(correlate_kernel, chunks, 1.0 / depth),
        grid_spec=pltpu.PrefetchScalarGridSpec(
            num_scalar_prefetch=1,
            grid=(steps,),
            in_specs=[whole if x.shape[0] == chans else own for x in arrays]
            + [pl.BlockSpec(memory_space=pl.ANY)] * len(before),
            out_specs=[out, out],
        ),
        out_shape=[shape, shape],
        input_output_aliases={1 + len(arrays) + j: j for j in range(len(before))},
        compiler_params=pltpu.CompilerParams(vmem_limit_bytes=VMEM),
        cost_estimate=pl.CostEstimate(
            flops=2 * chans // parts * 8 * inputs * 4 * inputs * depth,
            bytes_accessed=36 * 2**20 // parts,
            transcendentals=0,
        ),
        name="correlate",
    )(place, *arrays, *before)


def ring(size, distance):
    return [(i, (i + distance) % size) for i in range(size)]


def shards(voltages, window, table):
    in_dev, frames, length = voltages.shape
    n_freq, n_col = lax.axis_size("freq"), lax.axis_size("col")
    n_in = in_dev // CHUNKS
    back = [(i + 1, i) for i in range(n_freq - 1)]
    row, col = lax.axis_index("row"), lax.axis_index("col")
    up, down = ring(n_col, 1), ring(n_col, -1)

    halos = [lax.ppermute(voltages[q * n_in : (q + 1) * n_in], "freq", back) for q in range(CHUNKS)]
    sent, pieces = [None] * CHUNKS, [None] * CHUNKS

    def front(q, *earlier):
        out = channelize(q, n_in, voltages, halos[q], window, table, earlier)
        sent[q] = lax.all_to_all(out, "freq", split_axis=0, concat_axis=0, tiled=True)
        return out

    def gather(q, *earlier):
        pieces[q] = []
        for block in turn(sent[q], earlier, PARTS if q == CHUNKS - 1 else 1):
            below = lax.ppermute(block, "col", up)
            above = lax.ppermute(block, "col", down)
            if (q + len(pieces[q])) % 2 == 0:
                across = lax.ppermute(below, "col", up)
            else:
                across = lax.ppermute(above, "col", down)
            swapped = lax.ppermute(block, "row", ring(2, 1))
            pieces[q].append((block, below, above, across, swapped))

    front(0)
    gather(0, front(1))
    gather(1, front(2, pieces[0][0][0]))
    gather(2, front(3, pieces[1][0][0], *pieces[0][0][1:3]))
    gather(3, *pieces[1][0][1:3], *pieces[0][0][3:], pieces[2][0][0])
    place = jnp.stack([row, col, (col + 3) % 4, (col + 1) % 4, (col + 2) % 4]).astype(jnp.int32)
    outs = ()
    for part in range(PARTS):
        chosen = [p[part] if len(p) > 1 else p[0] for p in pieces]
        blocks = [chosen[q][d] for d in range(4) for q in range(CHUNKS)]
        swapped = [chosen[q][4] for q in range(CHUNKS)]
        outs = correlate(place, blocks, swapped, part, PARTS, outs)
    return tuple(outs)


def solution(mesh):
    n_freq = mesh.shape["freq"]

    def run(voltages, window):
        table = jnp.asarray(dft_table(voltages.shape[2], n_freq))
        return jax.shard_map(
            shards,
            mesh=mesh,
            in_specs=(P(("row", "col"), "freq", None), P(), P()),
            out_specs=(P("freq", "row", "col"), P("freq", "row", "col")),
            check_vma=False,
        )(voltages, window, table)

    return run
```

time: 284 us -> 242 us (0.85)
  local copies, waits for them, and re-layouts: 28.4 us -> 8.79 us
  starting transfers between devices: 73.7 us -> 63.2 us
  waiting for transfers between devices: 99.7 us -> 92 us
  Pallas kernels: 79.2 us -> 75.7 us
    ppermute x20 -> x24, waiting for transfers between devices: 93.3 us -> 61.6 us  [the longest x5 25.2 us: gather(): below = lax.ppermute(block, 'col', up)]
    all_to_all x4, waiting for transfers between devices: 6.35 us -> 30.4 us  [front(): lax.all_to_all(out, 'freq', split_axis=0, concat_axis=0, tiled=True)]
    unnamed x30 -> x20, local copies, waits for them, and re-layouts: 24.2 us -> 4.18 us
    ppermute x20 -> x24, starting transfers between devices: 37.9 us -> 29.2 us  [the longest x5 8.22 us: gather(): swapped = lax.ppermute(block, 'row', ring(2, 1))]
    pallas_call x1 -> x2, Pallas kernels: 25.6 us -> 19.1 us  [correlate(): pl.pallas_call(functools.partial(correlate_kernel, chunks, 1.0 / depth),...]
  transfers between devices with their start and end apart: 24 -> 28, of which waited for: 12 -> 11; matrix products, arithmetic and copies ran while one was open for 0% -> 0% of each run, Pallas kernels for 19% -> 27%
where the time goes in v2:
time: 242 us; the launch traced here: 241 us
  waiting for transfers between devices  92 us (38%)
  Pallas kernels  75.7 us (31%)
  starting transfers between devices  63.2 us (26%)
  local copies, waits for them, and re-layouts  8.79 us (4%)
    pallas_call x4, Pallas kernels, channelize(): pl.pallas_call(channelize_kernel, grid=(blocks,), in_specs=[pl.BlockSpec(...  39.9 us
    all_to_all x4, starting transfers between devices, front(): lax.all_to_all(out, 'freq', split_axis=0, concat_axis=0, tiled=True)  33.9 us
    all_to_all x4, waiting for transfers between devices, front(): lax.all_to_all(out, 'freq', split_axis=0, concat_axis=0, tiled=True)  30.4 us
    ppermute x5, waiting for transfers between devices, gather(): below = lax.ppermute(block, 'col', up)  25.2 us
    ppermute x5, waiting for transfers between devices, gather(): swapped = lax.ppermute(block, 'row', ring(2, 1))  19.5 us
    pallas_call x2, Pallas kernels, correlate(): pl.pallas_call(functools.partial(correlate_kernel, chunks, 1.0 / depth),...  19.1 us
    pallas_call x4, Pallas kernels, turn(): pl.pallas_call(functools.partial(turn_kernel, parts), in_specs=[vmem] + [...  16.7 us
    ppermute x3, waiting for transfers between devices, gather(): across = lax.ppermute(below, 'col', up)  12.4 us
  transfers between devices with their start and end apart: 28, of which 11 were waited for; matrix products, arithmetic and copies ran while one was open for 0% of the time, Pallas kernels for 27%

profile of v2, /device:TPU:0, one launch (start us, length us, event | category | flops | bytes accessed | tf_op | source)
XLA Modules:
  0.0 240.6 jit_solution(9332708635920051836)
XLA Ops:
  0.6 4.0 %fusion = (bf16[16,16,2048]{2,1,0:T(8,128)(2,1)}, bf16[16,16,2048]{2,1,0:T(8,128)(2,1)}, bf16[16,16,2048]{2,1,0:T(8,128)(2,1)S(1)}, bf16[16,16,2048]{2,1,0:T(8,128)(2,1)S(1)}) fusion(bf16[64,16,2048]{2,1,0:T(8,128)(2,1)} %v_ref.7), kind=kLoop, calls=%fused_computation | loop fusion | bytes 8388608 | tf_op jit(solution)/shard_map/slice | solution.py:204
  4.6 1.3 collective-permute-start
  5.9 1.3 collective-permute-start.1
  7.2 2.0 collective-permute-done.h_ref
  9.2 1.0 copy-done.9
  10.2 10.0 %channelize.4 = bf16[16,16,16,128]{3,2,1,0:T(8,128)(2,1)} custom-call(bf16[64,16,2048]{2,1,0:T(8,128)(2,1)} %v_ref.7, bf16[16,16,2048]{2,1,0:T(8,128)(2,1)} %copy-done.9, f32[16,2048]{1,0:T(8,128)} %w_ref.7, bf16[4,2048,512]{2,1,0:T(8,128)(2,1)} %constant.37.clone.t_ref), custom_call_target="tpu_custom_call" | custom-call | flops 100000000 | bytes 131072 | tf_op jit(solution)/shard_map/channelize/pallas_call | solution.py:69
  20.1 17.5 %all-to-all-start = ((bf16[16,16,16,128]{3,2,1,0:T(8,128)(2,1)}), bf16[16,16,16,128]{3,2,1,0:T(8,128)(2,1)S(1)}, u32[]{:S(2)}, u32[]{:S(2)}) async-start(bf16[16,16,16,128]{3,2,1,0:T(8,128)(2,1)} %channelize.4), calls=%async_computation | async-start | bytes 2097152 | tf_op jit(solution)/shard_map/all_to_all | solution.py:209
  37.6 1.3 collective-permute-start.2
  38.9 0.0 collective-permute-done.1.h_ref
  38.9 1.0 copy-done.8
  39.9 10.0 %channelize.5.refs_0_ = bf16[16,16,16,128]{3,2,1,0:T(8,128)(2,1)} custom-call(bf16[64,16,2048]{2,1,0:T(8,128)(2,1)} %v_ref.7, bf16[16,16,2048]{2,1,0:T(8,128)(2,1)} %copy-done.8, f32[16,2048]{1,0:T(8,128)} %w_ref.7, bf16[4,2048,512]{2,1,0:T(8,128)(2,1)} %constant.37.clone.t_ref), custom_call_target="tpu_custom_call" | custom-call | flops 100000000 | bytes 131072 | tf_op jit(solution)/shard_map/channelize/pallas_call | solution.py:69
  49.9 4.3 %all-to-all-done.x_ref = bf16[16,16,16,128]{3,2,1,0:T(8,128)(2,1)S(1)} async-done(((bf16[16,16,16,128]{3,2,1,0:T(8,128)(2,1)}), bf16[16,16,16,128]{3,2,1,0:T(8,128)(2,1)S(1)}, u32[]{:S(2)}, u32[]{:S(2)}) %all-to-all-start) | async-done | bytes 1048608 | tf_op jit(solution)/shard_map/all_to_all | solution.py:209
  54.2 4.3 %all-to-all-start.1 = ((bf16[16,16,16,128]{3,2,1,0:T(8,128)(2,1)}), bf16[16,16,16,128]{3,2,1,0:T(8,128)(2,1)}, u32[]{:S(2)}, u32[]{:S(2)}) async-start(bf16[16,16,16,128]{3,2,1,0:T(8,128)(2,1)} %channelize.5.refs_0_), calls=%async_computation.1 | async-start | bytes 2097152 | tf_op jit(solution)/shard_map/all_to_all | solution.py:209
  58.6 1.3 collective-permute-start.3
  59.9 4.2 %turn.4.refs_0_ = bf16[64,32,256]{2,1,0:T(8,128)(2,1)} custom-call(bf16[16,16,16,128]{3,2,1,0:T(8,128)(2,1)} %copy-done.3, bf16[16,16,16,128]{3,2,1,0:T(8,128)(2,1)} %channelize.5.refs_0_), custom_call_target="tpu_custom_call" | custom-call | flops 100000000 | bytes 131072 | tf_op jit(solution)/shard_map/turn/pallas_call | solution.py:115
  64.1 1.9 collective-permute-start.4
  66.0 2.1 collective-permute-start.5
  68.1 10.0 %channelize.6.refs_0_ = bf16[16,16,16,128]{3,2,1,0:T(8,128)(2,1)} custom-call(bf16[64,16,2048]{2,1,0:T(8,128)(2,1)} %v_ref.7, bf16[16,16,2048]{2,1,0:T(8,128)(2,1)} %collective-permute-done.2.h_ref, f32[16,2048]{1,0:T(8,128)} %w_ref.7, bf16[4,2048,512]{2,1,0:T(8,128)(2,1)} %constant.37.clone.t_ref, bf16[64,32,256]{2,1,0:T(8,128)(2,1)} %turn.4.refs_0_), custom_call_target="tpu_custom_call" | custom-call | flops 100000000 | bytes 131072 | tf_op jit(solution)/shard_map/channelize/pallas_call | solution.py:69
  78.1 4.2 %turn.5.refs_0_.refs_1_ = bf16[64,32,256]{2,1,0:T(8,128)(2,1)} custom-call(bf16[16,16,16,128]{3,2,1,0:T(8,128)(2,1)} %all-to-all-done.1.x_ref, bf16[16,16,16,128]{3,2,1,0:T(8,128)(2,1)} %channelize.6.refs_0_), custom_call_target="tpu_custom_call" | custom-call | flops 100000000 | bytes 131072 | tf_op jit(solution)/shard_map/turn/pallas_call | solution.py:115
  82.3 2.7 %collective-permute-start.7 = (bf16[64,32,256]{2,1,0:T(8,128)(2,1)}, bf16[64,32,256]{2,1,0:T(8,128)(2,1)}, u32[]{:S(2)}, u32[]{:S(2)}) collective-permute-start(bf16[64,32,256]{2,1,0:T(8,128)(2,1)} %turn.5.refs_0_.refs_1_), channel_id=1, source_target_pairs={{0,3},{1,0},{2,1},{3,2},{4,7},{5,4},{6,5},{7,6},{8,11},{9,8},{10,9... | collective-permute-start | bytes 3145736 | tf_op jit(solution)/shard_map/ppermute | solution.py:216
  85.0 5.8 %all-to-all-start.2 = ((bf16[16,16,16,128]{3,2,1,0:T(8,128)(2,1)}), bf16[16,16,16,128]{3,2,1,0:T(8,128)(2,1)}, u32[]{:S(2)}, u32[]{:S(2)}) async-start(bf16[16,16,16,128]{3,2,1,0:T(8,128)(2,1)} %channelize.6.refs_0_), calls=%async_computation.2 | async-start | bytes 2097152 | tf_op jit(solution)/shard_map/all_to_all | solution.py:209
  90.9 0.1 collective-permute-start.6
  91.0 2.8 %collective-permute-start.9 = (bf16[64,32,256]{2,1,0:T(8,128)(2,1)S(1)}, bf16[64,32,256]{2,1,0:T(8,128)(2,1)}, u32[]{:S(2)}, u32[]{:S(2)}) collective-permute-start(bf16[64,32,256]{2,1,0:T(8,128)(2,1)S(1)} %copy-done), channel_id=1, source_target_pairs={{0,4},{4,0},{1,5},{5,1},{2,6},{6,2},{3,7},{7,3},{8,12},{12,8},{9,1... | collective-permute-start | bytes 3145736 | tf_op jit(solution)/shard_map/ppermute | solution.py:221
  93.8 0.0 collective-permute-done.4.refs_1_.refs_4_
  93.8 0.0 collective-permute-start.8
  93.8 1.1 collective-permute-start.17
  94.9 0.2 copy-done.2
  95.1 10.0 %channelize.7.refs_0_ = bf16[16,16,16,128]{3,2,1,0:T(8,128)(2,1)} custom-call(bf16[64,16,2048]{2,1,0:T(8,128)(2,1)} %v_ref.7, bf16[16,16,2048]{2,1,0:T(8,128)(2,1)} %collective-permute-done.3.h_ref, f32[16,2048]{1,0:T(8,128)} %w_ref.7, bf16[4,2048,512]{2,1,0:T(8,128)(2,1)} %constant.37.clone.t_ref, bf16[64,32,256]{2,1,0:T(8,128)(2,1)} %turn.5.refs_0_.refs_1_, ...), custom_call_target="tpu_custom_call" | custom-call | flops 100000000 | bytes 131072 | tf_op jit(solution)/shard_map/channelize/pallas_call | solution.py:69
  105.1 2.9 %all-to-all-done.2.x_ref = bf16[16,16,16,128]{3,2,1,0:T(8,128)(2,1)} async-done(((bf16[16,16,16,128]{3,2,1,0:T(8,128)(2,1)}), bf16[16,16,16,128]{3,2,1,0:T(8,128)(2,1)}, u32[]{:S(2)}, u32[]{:S(2)}) %all-to-all-start.2) | async-done | bytes 1048608 | tf_op jit(solution)/shard_map/all_to_all | solution.py:209
  108.0 4.2 %turn.6.refs_4_.refs_2_ = bf16[64,32,256]{2,1,0:T(8,128)(2,1)} custom-call(bf16[16,16,16,128]{3,2,1,0:T(8,128)(2,1)} %all-to-all-done.2.x_ref, bf16[16,16,16,128]{3,2,1,0:T(8,128)(2,1)} %channelize.7.refs_0_), custom_call_target="tpu_custom_call" | custom-call | flops 100000000 | bytes 131072 | tf_op jit(solution)/shard_map/turn/pallas_call | solution.py:115
  112.2 2.5 %collective-permute-done.7.refs_1_.refs_9_ = bf16[64,32,256]{2,1,0:T(8,128)(2,1)} collective-permute-done((bf16[64,32,256]{2,1,0:T(8,128)(2,1)}, bf16[64,32,256]{2,1,0:T(8,128)(2,1)}, u32[]{:S(2)}, u32[]{:S(2)}) %collective-permute-start.7) | collective-permute-done | bytes 1048608 | tf_op jit(solution)/shard_map/ppermute | solution.py:216
  114.7 1.9 collective-permute-start.10
  116.6 6.3 %all-to-all-start.3 = ((bf16[16,16,16,128]{3,2,1,0:T(8,128)(2,1)}), bf16[16,16,16,128]{3,2,1,0:T(8,128)(2,1)S(1)}, u32[]{:S(2)}, u32[]{:S(2)}) async-start(bf16[16,16,16,128]{3,2,1,0:T(8,128)(2,1)} %channelize.7.refs_0_), calls=%async_computation.3 | async-start | bytes 2097152 | tf_op jit(solution)/shard_map/all_to_all | solution.py:209
  122.9 1.4 collective-permute-start.14
  124.3 5.2 %collective-permute-done.9.refs_3_.refs_16_ = bf16[64,32,256]{2,1,0:T(8,128)(2,1)} collective-permute-done((bf16[64,32,256]{2,1,0:T(8,128)(2,1)S(1)}, bf16[64,32,256]{2,1,0:T(8,128)(2,1)}, u32[]{:S(2)}, u32[]{:S(2)}) %collective-permute-start.9) | collective-permute-done | bytes 1048608 | tf_op jit(solution)/shard_map/ppermute | solution.py:221
  129.4 0.8 collective-permute-start.18
  130.2 10.7 %collective-permute-done.8.refs_2_.refs_12_ = bf16[64,32,256]{2,1,0:T(8,128)(2,1)} collective-permute-done((bf16[64,32,256]{2,1,0:T(8,128)(2,1)S(1)}, bf16[64,32,256]{2,1,0:T(8,128)(2,1)}, u32[]{:S(2)}, u32[]{:S(2)}) %collective-permute-start.8) | collective-permute-done | bytes 1048608 | tf_op jit(solution)/shard_map/ppermute | solution.py:218
  141.0 0.0 collective-permute-start.12
  141.0 23.1 %all-to-all-done.3.x_ref = bf16[16,16,16,128]{3,2,1,0:T(8,128)(2,1)S(1)} async-done(((bf16[16,16,16,128]{3,2,1,0:T(8,128)(2,1)}), bf16[16,16,16,128]{3,2,1,0:T(8,128)(2,1)S(1)}, u32[]{:S(2)}, u32[]{:S(2)}) %all-to-all-start.3) | async-done | bytes 1048608 | tf_op jit(solution)/shard_map/all_to_all | solution.py:209
  164.1 1.0 copy-done.4
  165.1 4.2 %turn.7 = (bf16[32,32,256]{2,1,0:T(8,128)(2,1)}, bf16[32,32,256]{2,1,0:T(8,128)(2,1)}) custom-call(bf16[16,16,16,128]{3,2,1,0:T(8,128)(2,1)} %copy-done.4, bf16[64,32,256]{2,1,0:T(8,128)(2,1)} %collective-permute-done.6.refs_0_.refs_5_, bf16[64,32,256]{2,1,0:T(8,128)(2,1)} %collective-permute-done.7.refs_1_.refs_9_, ...), custom_call_target="tpu_custom_call" | custom-call | flops 100000000 | bytes 131072 | tf_op jit(solution)/shard_map/turn/pallas_call | solution.py:115
  169.2 0.4 collective-permute-start.21
  169.6 1.6 collective-permute-start.15
  171.3 0.0 collective-permute-done.14.refs_13_
  171.3 0.1 collective-permute-start.11
  171.3 14.3 %collective-permute-done.18.refs_18_ = bf16[64,32,256]{2,1,0:T(8,128)(2,1)S(1)} collective-permute-done((bf16[64,32,256]{2,1,0:T(8,128)(2,1)}, bf16[64,32,256]{2,1,0:T(8,128)(2,1)S(1)}, u32[]{:S(2)}, u32[]{:S(2)}) %collective-permute-start.18) | collective-permute-done | bytes 1048608 | tf_op jit(solution)/shard_map/ppermute | solution.py:221
  185.6 0.8 collective-permute-start.23
  186.4 0.0 collective-permute-done.12.refs_10_
  186.4 0.0 collective-permute-start.20
  186.5 0.0 collective-permute-done.21.refs_11_
  186.5 3.2 %collective-permute-start.22 = (bf16[32,32,256]{2,1,0:T(8,128)(2,1)}, bf16[32,32,256]{2,1,0:T(8,128)(2,1)}, u32[]{:S(2)}, u32[]{:S(2)}) collective-permute-start(bf16[32,32,256]{2,1,0:T(8,128)(2,1)} %collective-permute-done.21.refs_11_), channel_id=1, source_target_pairs={{0,3},{1,0},{2,1},{3,2},{4,7},{5,4},{6,5},{7,6},{8,11},{9,8},{10,9... | collective-permute-start | bytes 1572872 | tf_op jit(solution)/shard_map/ppermute | solution.py:220
  189.7 18.8 %collective-permute-done.11.refs_7_ = bf16[32,32,256]{2,1,0:T(8,128)(2,1)} collective-permute-done((bf16[32,32,256]{2,1,0:T(8,128)(2,1)}, bf16[32,32,256]{2,1,0:T(8,128)(2,1)}, u32[]{:S(2)}, u32[]{:S(2)}) %collective-permute-start.11) | collective-permute-done | bytes 524320 | tf_op jit(solution)/shard_map/ppermute | solution.py:215
  208.5 2.7 %collective-permute-start.19 = (bf16[32,32,256]{2,1,0:T(8,128)(2,1)}, bf16[32,32,256]{2,1,0:T(8,128)(2,1)}, u32[]{:S(2)}, u32[]{:S(2)}) collective-permute-start(bf16[32,32,256]{2,1,0:T(8,128)(2,1)} %get-tuple-element.6.refs_3_), channel_id=1, source_target_pairs={{0,4},{4,0},{1,5},{5,1},{2,6},{6,2},{3,7},{7,3},{8,12},{12,8},{9,1... | collective-permute-start | bytes 1572872 | tf_op jit(solution)/shard_map/ppermute | solution.py:221
  211.2 0.0 collective-permute-done.23.refs_19_
  211.2 0.0 collective-permute-start.13
  211.2 6.4 %collective-permute-done.20.refs_7_ = bf16[32,32,256]{2,1,0:T(8,128)(2,1)} collective-permute-done((bf16[32,32,256]{2,1,0:T(8,128)(2,1)}, bf16[32,32,256]{2,1,0:T(8,128)(2,1)}, u32[]{:S(2)}, u32[]{:S(2)}) %collective-permute-start.20) | collective-permute-done | bytes 524320 | tf_op jit(solution)/shard_map/ppermute | solution.py:215
  217.6 0.4 collective-permute-start.16
  218.0 0.6 stack.23.place
  218.6 1.0 copy-done.7
  219.6 9.5 %correlate.2 = (f32[64,256,128]{2,1,0:T(8,128)}, f32[64,256,128]{2,1,0:T(8,128)}) custom-call(s32[5]{0:T(128)} %stack.23.place, bf16[64,32,256]{2,1,0:T(8,128)(2,1)} %turn.4.refs_0_, bf16[64,32,256]{2,1,0:T(8,128)(2,1)} %turn.5.refs_0_.refs_1_, bf16[64,32,256]{2,1,0:T(8,128)(2,1)} %turn.6.refs_4_.refs_2_, bf16[32,32,256]{2,1,0:T(8,128)(2,1)} %get-tuple-element.7.refs_3_, ...), custom_call_target="tpu_custom_call" | custom-call | flops 2147483648 | bytes 18874368 | tf_op jit(solution)/shard_map/correlate/pallas_call | solution.py:171
  229.2 0.0 collective-permute-done.19.refs_19_
  229.2 0.0 collective-permute-done.13.refs_11_
  229.2 1.7 collective-permute-done.16.refs_15_
  230.9 9.5 %correlate.3 = (f32[64,256,128]{2,1,0:T(8,128)}, f32[64,256,128]{2,1,0:T(8,128)}) custom-call(s32[5]{0:T(128)} %stack.23.place, bf16[64,32,256]{2,1,0:T(8,128)(2,1)} %turn.4.refs_0_, bf16[64,32,256]{2,1,0:T(8,128)(2,1)} %turn.5.refs_0_.refs_1_, bf16[64,32,256]{2,1,0:T(8,128)(2,1)} %turn.6.refs_4_.refs_2_, ...), custom_call_target="tpu_custom_call", output_to_operand_aliasing={{0}: (21, {}), {1}: (22, {})} | custom-call | flops 2147483648 | bytes 18874368 | tf_op jit(solution)/shard_map/correlate/pallas_call | solution.py:171
  (24 shorter events, 0.1 us)
Async XLA Ops:
  4.6 4.5 %collective-permute-start = (bf16[16,16,2048]{2,1,0:T(8,128)(2,1)S(1)}, bf16[16,16,2048]{2,1,0:T(8,128)(2,1)S(1)}, u32[]{:S(2)}, u32[]{:S(2)}) collective-permute-start(bf16[16,16,2048]{2,1,0:T(8,128)(2,1)S(1)} %get-tuple-element.13), channel_id=1, source_target_pairs={{8,0},{16,8},{24,16},{32,24},{40,32},{48,40},{56,48},{64,56},{72,6... | collective-permute-start | bytes 3145736 | tf_op jit(solution)/shard_map/ppermute | solution.py:204
  5.9 33.0 %collective-permute-start.1 = (bf16[16,16,2048]{2,1,0:T(8,128)(2,1)S(1)}, bf16[16,16,2048]{2,1,0:T(8,128)(2,1)S(1)}, u32[]{:S(2)}, u32[]{:S(2)}) collective-permute-start(bf16[16,16,2048]{2,1,0:T(8,128)(2,1)S(1)} %get-tuple-element.12), channel_id=1, source_target_pairs={{8,0},{16,8},{24,16},{32,24},{40,32},{48,40},{56,48},{64,56},{72,6... | collective-permute-start | bytes 3145736 | tf_op jit(solution)/shard_map/ppermute | solution.py:204
  9.2 1.0 copy-start.9
  20.1 34.1 %all-to-all-start = ((bf16[16,16,16,128]{3,2,1,0:T(8,128)(2,1)}), bf16[16,16,16,128]{3,2,1,0:T(8,128)(2,1)S(1)}, u32[]{:S(2)}, u32[]{:S(2)}) async-start(bf16[16,16,16,128]{3,2,1,0:T(8,128)(2,1)} %channelize.4), calls=%async_computation | async-start | bytes 2097152 | tf_op jit(solution)/shard_map/all_to_all | solution.py:209
  37.6 30.5 %collective-permute-start.2 = (bf16[16,16,2048]{2,1,0:T(8,128)(2,1)}, bf16[16,16,2048]{2,1,0:T(8,128)(2,1)}, u32[]{:S(2)}, u32[]{:S(2)}) collective-permute-start(bf16[16,16,2048]{2,1,0:T(8,128)(2,1)} %get-tuple-element.11), channel_id=1, source_target_pairs={{8,0},{16,8},{24,16},{32,24},{40,32},{48,40},{56,48},{64,56},{72,6... | collective-permute-start | bytes 3145736 | tf_op jit(solution)/shard_map/ppermute | solution.py:204
  38.9 1.0 copy-start.8
  54.2 5.6 %copy-start.3 = (bf16[16,16,16,128]{3,2,1,0:T(8,128)(2,1)}, bf16[16,16,16,128]{3,2,1,0:T(8,128)(2,1)S(1)}, u32[]{:S(2)}) copy-start(bf16[16,16,16,128]{3,2,1,0:T(8,128)(2,1)S(1)} %all-to-all-done.x_ref) | copy-start | bytes 3145732
  54.2 23.9 %all-to-all-start.1 = ((bf16[16,16,16,128]{3,2,1,0:T(8,128)(2,1)}), bf16[16,16,16,128]{3,2,1,0:T(8,128)(2,1)}, u32[]{:S(2)}, u32[]{:S(2)}) async-start(bf16[16,16,16,128]{3,2,1,0:T(8,128)(2,1)} %channelize.5.refs_0_), calls=%async_computation.1 | async-start | bytes 2097152 | tf_op jit(solution)/shard_map/all_to_all | solution.py:209
  58.6 32.4 %collective-permute-start.3 = (bf16[16,16,2048]{2,1,0:T(8,128)(2,1)}, bf16[16,16,2048]{2,1,0:T(8,128)(2,1)}, u32[]{:S(2)}, u32[]{:S(2)}) collective-permute-start(bf16[16,16,2048]{2,1,0:T(8,128)(2,1)} %get-tuple-element.10), channel_id=1, source_target_pairs={{8,0},{16,8},{24,16},{32,24},{40,32},{48,40},{56,48},{64,56},{72,6... | collective-permute-start | bytes 3145736 | tf_op jit(solution)/shard_map/ppermute | solution.py:204
  64.1 26.9 %copy-start = (bf16[64,32,256]{2,1,0:T(8,128)(2,1)S(1)}, bf16[64,32,256]{2,1,0:T(8,128)(2,1)}, u32[]{:S(2)}) copy-start(bf16[64,32,256]{2,1,0:T(8,128)(2,1)} %turn.4.refs_0_) | copy-start | bytes 3145732
  64.1 29.7 %collective-permute-start.4 = (bf16[64,32,256]{2,1,0:T(8,128)(2,1)}, bf16[64,32,256]{2,1,0:T(8,128)(2,1)S(1)}, u32[]{:S(2)}, u32[]{:S(2)}) collective-permute-start(bf16[64,32,256]{2,1,0:T(8,128)(2,1)} %turn.4.refs_0_), channel_id=1, source_target_pairs={{0,1},{1,2},{2,3},{3,0},{4,5},{5,6},{6,7},{7,4},{8,9},{9,10},{10,1... | collective-permute-start | bytes 3145736 | tf_op jit(solution)/shard_map/ppermute | solution.py:215
  66.0 27.8 %collective-permute-start.5 = (bf16[64,32,256]{2,1,0:T(8,128)(2,1)}, bf16[64,32,256]{2,1,0:T(8,128)(2,1)S(1)}, u32[]{:S(2)}, u32[]{:S(2)}) collective-permute-start(bf16[64,32,256]{2,1,0:T(8,128)(2,1)} %turn.4.refs_0_), channel_id=1, source_target_pairs={{0,3},{1,0},{2,1},{3,2},{4,7},{5,4},{6,5},{7,6},{8,11},{9,8},{10,9... | collective-permute-start | bytes 3145736 | tf_op jit(solution)/shard_map/ppermute | solution.py:216
  82.3 32.4 %collective-permute-start.7 = (bf16[64,32,256]{2,1,0:T(8,128)(2,1)}, bf16[64,32,256]{2,1,0:T(8,128)(2,1)}, u32[]{:S(2)}, u32[]{:S(2)}) collective-permute-start(bf16[64,32,256]{2,1,0:T(8,128)(2,1)} %turn.5.refs_0_.refs_1_), channel_id=1, source_target_pairs={{0,3},{1,0},{2,1},{3,2},{4,7},{5,4},{6,5},{7,6},{8,11},{9,8},{10,9... | collective-permute-start | bytes 3145736 | tf_op jit(solution)/shard_map/ppermute | solution.py:216
  85.0 23.0 %all-to-all-start.2 = ((bf16[16,16,16,128]{3,2,1,0:T(8,128)(2,1)}), bf16[16,16,16,128]{3,2,1,0:T(8,128)(2,1)}, u32[]{:S(2)}, u32[]{:S(2)}) async-start(bf16[16,16,16,128]{3,2,1,0:T(8,128)(2,1)} %channelize.6.refs_0_), calls=%async_computation.2 | async-start | bytes 2097152 | tf_op jit(solution)/shard_map/all_to_all | solution.py:209
  90.9 32.0 %collective-permute-start.6 = (bf16[64,32,256]{2,1,0:T(8,128)(2,1)}, bf16[64,32,256]{2,1,0:T(8,128)(2,1)}, u32[]{:S(2)}, u32[]{:S(2)}) collective-permute-start(bf16[64,32,256]{2,1,0:T(8,128)(2,1)} %turn.5.refs_0_.refs_1_), channel_id=1, source_target_pairs={{0,1},{1,2},{2,3},{3,0},{4,5},{5,6},{6,7},{7,4},{8,9},{9,10},{10,1... | collective-permute-start | bytes 3145736 | tf_op jit(solution)/shard_map/ppermute | solution.py:215
  91.0 38.4 %collective-permute-start.9 = (bf16[64,32,256]{2,1,0:T(8,128)(2,1)S(1)}, bf16[64,32,256]{2,1,0:T(8,128)(2,1)}, u32[]{:S(2)}, u32[]{:S(2)}) collective-permute-start(bf16[64,32,256]{2,1,0:T(8,128)(2,1)S(1)} %copy-done), channel_id=1, source_target_pairs={{0,4},{4,0},{1,5},{5,1},{2,6},{6,2},{3,7},{7,3},{8,12},{12,8},{9,1... | collective-permute-start | bytes 3145736 | tf_op jit(solution)/shard_map/ppermute | solution.py:221
  93.8 1.1 copy-start.1
  93.8 47.1 %collective-permute-start.8 = (bf16[64,32,256]{2,1,0:T(8,128)(2,1)S(1)}, bf16[64,32,256]{2,1,0:T(8,128)(2,1)}, u32[]{:S(2)}, u32[]{:S(2)}) collective-permute-start(bf16[64,32,256]{2,1,0:T(8,128)(2,1)S(1)} %collective-permute-done.4.refs_1_.refs_4_), channel_id=1, source_target_pairs={{0,1},{1,2},{2,3},{3,0},{4,5},{5,6},{6,7},{7,4},{8,9},{9,10},{10,1... | collective-permute-start | bytes 3145736 | tf_op jit(solution)/shard_map/ppermute | solution.py:218
  93.8 1.3 copy-start.2
  93.8 75.4 %collective-permute-start.17 = (bf16[64,32,256]{2,1,0:T(8,128)(2,1)}, bf16[64,32,256]{2,1,0:T(8,128)(2,1)}, u32[]{:S(2)}, u32[]{:S(2)}) collective-permute-start(bf16[64,32,256]{2,1,0:T(8,128)(2,1)} %turn.5.refs_0_.refs_1_), channel_id=1, source_target_pairs={{0,4},{4,0},{1,5},{5,1},{2,6},{6,2},{3,7},{7,3},{8,12},{12,8},{9,1... | collective-permute-start | bytes 3145736 | tf_op jit(solution)/shard_map/ppermute | solution.py:221
  114.7 54.9 %collective-permute-start.10 = (bf16[64,32,256]{2,1,0:T(8,128)(2,1)}, bf16[64,32,256]{2,1,0:T(8,128)(2,1)}, u32[]{:S(2)}, u32[]{:S(2)}) collective-permute-start(bf16[64,32,256]{2,1,0:T(8,128)(2,1)} %turn.6.refs_4_.refs_2_), channel_id=1, source_target_pairs={{0,1},{1,2},{2,3},{3,0},{4,5},{5,6},{6,7},{7,4},{8,9},{9,10},{10,1... | collective-permute-start | bytes 3145736 | tf_op jit(solution)/shard_map/ppermute | solution.py:215
  116.6 47.5 %all-to-all-start.3 = ((bf16[16,16,16,128]{3,2,1,0:T(8,128)(2,1)}), bf16[16,16,16,128]{3,2,1,0:T(8,128)(2,1)S(1)}, u32[]{:S(2)}, u32[]{:S(2)}) async-start(bf16[16,16,16,128]{3,2,1,0:T(8,128)(2,1)} %channelize.7.refs_0_), calls=%async_computation.3 | async-start | bytes 2097152 | tf_op jit(solution)/shard_map/all_to_all | solution.py:209
  122.9 48.3 %collective-permute-start.14 = (bf16[64,32,256]{2,1,0:T(8,128)(2,1)}, bf16[64,32,256]{2,1,0:T(8,128)(2,1)}, u32[]{:S(2)}, u32[]{:S(2)}) collective-permute-start(bf16[64,32,256]{2,1,0:T(8,128)(2,1)} %collective-permute-done.7.refs_1_.refs_9_), channel_id=1, source_target_pairs={{0,3},{1,0},{2,1},{3,2},{4,7},{5,4},{6,5},{7,6},{8,11},{9,8},{10,9... | collective-permute-start | bytes 3145736 | tf_op jit(solution)/shard_map/ppermute | solution.py:220
  129.4 56.2 %collective-permute-start.18 = (bf16[64,32,256]{2,1,0:T(8,128)(2,1)}, bf16[64,32,256]{2,1,0:T(8,128)(2,1)S(1)}, u32[]{:S(2)}, u32[]{:S(2)}) collective-permute-start(bf16[64,32,256]{2,1,0:T(8,128)(2,1)} %turn.6.refs_4_.refs_2_), channel_id=1, source_target_pairs={{0,4},{4,0},{1,5},{5,1},{2,6},{6,2},{3,7},{7,3},{8,12},{12,8},{9,1... | collective-permute-start | bytes 3145736 | tf_op jit(solution)/shard_map/ppermute | solution.py:221
  141.0 45.5 %collective-permute-start.12 = (bf16[64,32,256]{2,1,0:T(8,128)(2,1)}, bf16[64,32,256]{2,1,0:T(8,128)(2,1)S(1)}, u32[]{:S(2)}, u32[]{:S(2)}) collective-permute-start(bf16[64,32,256]{2,1,0:T(8,128)(2,1)} %turn.6.refs_4_.refs_2_), channel_id=1, source_target_pairs={{0,3},{1,0},{2,1},{3,2},{4,7},{5,4},{6,5},{7,6},{8,11},{9,8},{10,9... | collective-permute-start | bytes 3145736 | tf_op jit(solution)/shard_map/ppermute | solution.py:216
  164.1 1.0 copy-start.4
  169.2 17.2 %collective-permute-start.21 = (bf16[32,32,256]{2,1,0:T(8,128)(2,1)}, bf16[32,32,256]{2,1,0:T(8,128)(2,1)}, u32[]{:S(2)}, u32[]{:S(2)}) collective-permute-start(bf16[32,32,256]{2,1,0:T(8,128)(2,1)} %get-tuple-element.7.refs_3_), channel_id=1, source_target_pairs={{0,3},{1,0},{2,1},{3,2},{4,7},{5,4},{6,5},{7,6},{8,11},{9,8},{10,9... | collective-permute-start | bytes 1572872 | tf_op jit(solution)/shard_map/ppermute | solution.py:216
  169.6 49.0 %collective-permute-start.15 = (bf16[64,32,256]{2,1,0:T(8,128)(2,1)}, bf16[64,32,256]{2,1,0:T(8,128)(2,1)S(1)}, u32[]{:S(2)}, u32[]{:S(2)}) collective-permute-start(bf16[64,32,256]{2,1,0:T(8,128)(2,1)} %collective-permute-done.10.refs_6_), channel_id=1, source_target_pairs={{0,1},{1,2},{2,3},{3,0},{4,5},{5,6},{6,7},{7,4},{8,9},{9,10},{10,1... | collective-permute-start | bytes 3145736 | tf_op jit(solution)/shard_map/ppermute | solution.py:218
  171.3 37.2 %collective-permute-start.11 = (bf16[32,32,256]{2,1,0:T(8,128)(2,1)}, bf16[32,32,256]{2,1,0:T(8,128)(2,1)}, u32[]{:S(2)}, u32[]{:S(2)}) collective-permute-start(bf16[32,32,256]{2,1,0:T(8,128)(2,1)} %get-tuple-element.6.refs_3_), channel_id=1, source_target_pairs={{0,1},{1,2},{2,3},{3,0},{4,5},{5,6},{6,7},{7,4},{8,9},{9,10},{10,1... | collective-permute-start | bytes 1572872 | tf_op jit(solution)/shard_map/ppermute | solution.py:215
  185.6 33.0 %copy-start.5 = (bf16[64,32,256]{2,1,0:T(8,128)(2,1)}, bf16[64,32,256]{2,1,0:T(8,128)(2,1)S(1)}, u32[]{:S(2)}) copy-start(bf16[64,32,256]{2,1,0:T(8,128)(2,1)S(1)} %collective-permute-done.18.refs_18_) | copy-start | bytes 3145732
  185.6 25.6 %collective-permute-start.23 = (bf16[32,32,256]{2,1,0:T(8,128)(2,1)}, bf16[32,32,256]{2,1,0:T(8,128)(2,1)}, u32[]{:S(2)}, u32[]{:S(2)}) collective-permute-start(bf16[32,32,256]{2,1,0:T(8,128)(2,1)} %get-tuple-element.7.refs_3_), channel_id=1, source_target_pairs={{0,4},{4,0},{1,5},{5,1},{2,6},{6,2},{3,7},{7,3},{8,12},{12,8},{9,1... | collective-permute-start | bytes 1572872 | tf_op jit(solution)/shard_map/ppermute | solution.py:221
  186.4 32.2 %copy-start.6 = (bf16[64,32,256]{2,1,0:T(8,128)(2,1)}, bf16[64,32,256]{2,1,0:T(8,128)(2,1)S(1)}, u32[]{:S(2)}) copy-start(bf16[64,32,256]{2,1,0:T(8,128)(2,1)S(1)} %collective-permute-done.12.refs_10_) | copy-start | bytes 3145732
  186.4 31.1 %collective-permute-start.20 = (bf16[32,32,256]{2,1,0:T(8,128)(2,1)}, bf16[32,32,256]{2,1,0:T(8,128)(2,1)}, u32[]{:S(2)}, u32[]{:S(2)}) collective-permute-start(bf16[32,32,256]{2,1,0:T(8,128)(2,1)} %get-tuple-element.7.refs_3_), channel_id=1, source_target_pairs={{0,1},{1,2},{2,3},{3,0},{4,5},{5,6},{6,7},{7,4},{8,9},{9,10},{10,1... | collective-permute-start | bytes 1572872 | tf_op jit(solution)/shard_map/ppermute | solution.py:215
  186.5 32.1 %collective-permute-start.22 = (bf16[32,32,256]{2,1,0:T(8,128)(2,1)}, bf16[32,32,256]{2,1,0:T(8,128)(2,1)}, u32[]{:S(2)}, u32[]{:S(2)}) collective-permute-start(bf16[32,32,256]{2,1,0:T(8,128)(2,1)} %collective-permute-done.21.refs_11_), channel_id=1, source_target_pairs={{0,3},{1,0},{2,1},{3,2},{4,7},{5,4},{6,5},{7,6},{8,11},{9,8},{10,9... | collective-permute-start | bytes 1572872 | tf_op jit(solution)/shard_map/ppermute | solution.py:220
  208.5 20.7 %collective-permute-start.19 = (bf16[32,32,256]{2,1,0:T(8,128)(2,1)}, bf16[32,32,256]{2,1,0:T(8,128)(2,1)}, u32[]{:S(2)}, u32[]{:S(2)}) collective-permute-start(bf16[32,32,256]{2,1,0:T(8,128)(2,1)} %get-tuple-element.6.refs_3_), channel_id=1, source_target_pairs={{0,4},{4,0},{1,5},{5,1},{2,6},{6,2},{3,7},{7,3},{8,12},{12,8},{9,1... | collective-permute-start | bytes 1572872 | tf_op jit(solution)/shard_map/ppermute | solution.py:221
  211.2 18.0 %collective-permute-start.13 = (bf16[32,32,256]{2,1,0:T(8,128)(2,1)}, bf16[32,32,256]{2,1,0:T(8,128)(2,1)}, u32[]{:S(2)}, u32[]{:S(2)}) collective-permute-start(bf16[32,32,256]{2,1,0:T(8,128)(2,1)} %get-tuple-element.6.refs_3_), channel_id=1, source_target_pairs={{0,3},{1,0},{2,1},{3,2},{4,7},{5,4},{6,5},{7,6},{8,11},{9,8},{10,9... | collective-permute-start | bytes 1572872 | tf_op jit(solution)/shard_map/ppermute | solution.py:216
  217.6 13.3 %collective-permute-start.16 = (bf16[32,32,256]{2,1,0:T(8,128)(2,1)}, bf16[32,32,256]{2,1,0:T(8,128)(2,1)}, u32[]{:S(2)}, u32[]{:S(2)}) collective-permute-start(bf16[32,32,256]{2,1,0:T(8,128)(2,1)} %collective-permute-done.11.refs_7_), channel_id=1, source_target_pairs={{0,1},{1,2},{2,3},{3,0},{4,5},{5,6},{6,7},{7,4},{8,9},{9,10},{10,1... | collective-permute-start | bytes 1572872 | tf_op jit(solution)/shard_map/ppermute | solution.py:218
  218.6 1.0 copy-start.7

commit v3 on v2

v3 whole, which is shorter than its diff:
```python
import functools
import math

import jax
import jax.numpy as jnp
import ml_dtypes
import numpy as np
from jax import lax
from jax.experimental import pallas as pl
from jax.experimental.pallas import tpu as pltpu
from jax.sharding import PartitionSpec as P

LANES = 128
CHUNKS = 4
PARTS = 2
COPIES = (1, 1, 1, 2)
COLS = 512
SHORT = pl.CostEstimate(flops=10**8, bytes_accessed=2**17, transcendentals=0)
VMEM = 56 * 2**20


def dft_table(length, groups):
    half = length // 2
    base = np.arange(length) * (2.0 * math.pi / length)
    cosine = np.cos(base) / math.sqrt(length)
    sine = -np.sin(base) / math.sqrt(length)
    phase = np.arange(length)[:, None] * np.arange(half)[None, :] % length
    parts = np.stack([cosine[phase], sine[phase]], axis=1)
    parts = parts.reshape(length, 2, groups, half // groups).transpose(0, 2, 1, 3)
    blocks = parts.reshape(length, length // COLS, COLS).transpose(1, 0, 2)
    return blocks.astype(ml_dtypes.bfloat16)


def channelize_kernel(v_ref, h_ref, w_ref, t_ref, *refs):
    u_ref, ext, acc, filt = refs[-4:]
    n_in, frames, length = v_ref.shape
    taps = w_ref.shape[0]
    depth = 2 * frames

    @pl.when(pl.program_id(0) == 0)
    def _():
        def one_tile(t, carry):
            lanes = pl.ds(pl.multiple_of(t * LANES, LANES), LANES)
            for i in range(n_in):
                ext[pl.ds(i * depth, frames), :] = v_ref[i, :, lanes].astype(jnp.float32)
                ext[pl.ds(i * depth + frames, frames), :] = h_ref[i, :, lanes].astype(jnp.float32)
            weights = [jnp.broadcast_to(w_ref[pl.ds(k, 1), lanes], (8, LANES)) for k in range(taps)]
            for i in range(n_in):
                for s in range(0, frames, 8):
                    at = i * depth + s
                    total = weights[0] * ext[pl.ds(at, 8), :]
                    for k in range(1, taps):
                        total = total + weights[k] * ext[pl.ds(at + k, 8), :]
                    acc[pl.ds(i * frames + s, 8), :] = total
            filt[:, lanes] = acc[...].astype(jnp.bfloat16)
            return carry

        lax.fori_loop(0, length // LANES, one_tile, 0)

    out = jnp.dot(filt[...], t_ref[0], preferred_element_type=jnp.float32)
    out = out.astype(jnp.bfloat16)
    for j in range(u_ref.shape[0]):
        for row in range(u_ref.shape[1]):
            u_ref[j, row] = out[:, j * LANES : (j + 1) * LANES].reshape(n_in, frames, LANES)


def channelize(n_in, voltages, v_at, halo, window, table, copies, earlier):
    frames, length = voltages.shape[1:]
    blocks = table.shape[0]
    rows = n_in * frames
    return pl.pallas_call(
        channelize_kernel,
        grid=(blocks,),
        in_specs=[
            pl.BlockSpec((n_in, frames, length), lambda b: (v_at, 0, 0)),
            pl.BlockSpec((n_in, frames, length), lambda b: (0, 0, 0)),
            pl.BlockSpec(window.shape, lambda b: (0, 0)),
            pl.BlockSpec((1, length, COLS), lambda b: (b, 0, 0)),
            *[pl.BlockSpec(memory_space=pl.ANY)] * len(earlier),
        ],
        out_specs=pl.BlockSpec((COLS // LANES, copies, n_in, frames, LANES), lambda b: (b, 0, 0, 0, 0)),
        out_shape=jax.ShapeDtypeStruct((length // LANES, copies, n_in, frames, LANES), jnp.bfloat16),
        scratch_shapes=[
            pltpu.VMEM((2 * rows, LANES), jnp.float32),
            pltpu.VMEM((rows, LANES), jnp.float32),
            pltpu.VMEM((rows, length), jnp.bfloat16),
        ],
        compiler_params=pltpu.CompilerParams(vmem_limit_bytes=VMEM),
        cost_estimate=SHORT,
        name="channelize",
    )(voltages, halo, window, table, *earlier)


def turn_kernel(place, x_ref, *refs):
    g_ref, scr = refs[-2:]
    devices, _, n_in, frames, lanes = x_ref.shape
    chans = lanes // 2
    depth = devices * frames
    for h in range(depth // LANES):
        for i in range(n_in):
            piece = x_ref[h * LANES // frames : (h + 1) * LANES // frames, 0, i, :, :]
            piece = piece.reshape(LANES, lanes).astype(jnp.float32).T
            scr[h, pl.ds(i, chans, stride=2 * n_in), :] = piece[:chans]
            scr[h, pl.ds(n_in + i, chans, stride=2 * n_in), :] = piece[chans:]
        rows = scr[h].reshape(chans, 2 * n_in, LANES)
        g_ref[:, :, h * LANES : (h + 1) * LANES] = rows.astype(jnp.bfloat16)


def turn(received, row_of, place, earlier):
    devices, _, n_in, frames, lanes = received.shape
    chans, depth = lanes // 2, devices * frames
    return pl.pallas_call(
        turn_kernel,
        grid_spec=pltpu.PrefetchScalarGridSpec(
            num_scalar_prefetch=1,
            grid=(1,),
            in_specs=[pl.BlockSpec((devices, 1, n_in, frames, lanes), lambda b, place: (0, row_of(place), 0, 0, 0))]
            + [pl.BlockSpec(memory_space=pl.ANY)] * len(earlier),
            out_specs=pl.BlockSpec((chans, 2 * n_in, depth), lambda b, place: (0, 0, 0)),
            scratch_shapes=[pltpu.VMEM((depth // LANES, chans * 2 * n_in, LANES), jnp.float32)],
        ),
        out_shape=jax.ShapeDtypeStruct((chans, 2 * n_in, depth), jnp.bfloat16),
        compiler_params=pltpu.CompilerParams(vmem_limit_bytes=VMEM),
        cost_estimate=SHORT,
        name="turn",
    )(place, received, *earlier)


def correlate_kernel(chunks, scale, place, *refs):
    blocks, far_refs = refs[: 4 * chunks], refs[4 * chunks : 5 * chunks]
    near_refs = blocks[:chunks]
    re_ref, im_ref = refs[-2:]
    chans, twice, depth = blocks[0].shape
    n_in = twice // 2
    inputs = n_in * chunks
    half = 2 * inputs

    def channels(lower, upper):
        for ch in range(chans):
            partner = [ref[ch, part] for part in (slice(0, n_in), slice(n_in, twice)) for ref in (*lower, *upper)]
            partner = jnp.concatenate(partner, axis=0)
            first = jnp.concatenate([ref[ch] for ref in blocks], axis=0)
            products = lax.dot_general(
                first, partner, (((1,), (1,)), ((), ())), preferred_element_type=jnp.float32
            )
            for d in range(4):
                at = pl.multiple_of(place[1 + d] * inputs, inputs)
                for q in range(chunks):
                    start = (d * chunks + q) * twice
                    re = products[start : start + n_in]
                    im = products[start + n_in : start + twice]
                    rows = pl.ds(at + q * n_in, n_in)
                    re_ref[ch, rows, :] = (re[:, :half] + im[:, half:]) * scale
                    im_ref[ch, rows, :] = (im[:, :half] - re[:, half:]) * scale

    pl.when(place[0] == 0)(lambda: channels(near_refs, far_refs))
    pl.when(place[0] == 1)(lambda: channels(far_refs, near_refs))


def correlate(place, gathered, far, part, parts, before, step=8):
    chunks = len(far)
    chans, twice, depth = far[0].shape
    inputs = twice // 2 * chunks
    steps = chans // parts // step
    start = part * steps
    whole = pl.BlockSpec((step, twice, depth), lambda b, place: (b + start, 0, 0))
    own = pl.BlockSpec((step, twice, depth), lambda b, place: (b, 0, 0))
    out = pl.BlockSpec((step, 4 * inputs, 2 * inputs), lambda b, place: (b + start, 0, 0))
    shape = jax.ShapeDtypeStruct((chans, 4 * inputs, 2 * inputs), jnp.float32)
    arrays = [x for group in gathered for x in group] + far
    return pl.pallas_call(
        functools.partial(correlate_kernel, chunks, 1.0 / depth),
        grid_spec=pltpu.PrefetchScalarGridSpec(
            num_scalar_prefetch=1,
            grid=(steps,),
            in_specs=[whole if x.shape[0] == chans else own for x in arrays]
            + [pl.BlockSpec(memory_space=pl.ANY)] * len(before),
            out_specs=[out, out],
        ),
        out_shape=[shape, shape],
        input_output_aliases={1 + len(arrays) + j: j for j in range(len(before))},
        compiler_params=pltpu.CompilerParams(vmem_limit_bytes=VMEM),
        cost_estimate=SHORT,
        name="correlate",
    )(place, *arrays, *before)


def ring(size, distance):
    return [(i, (i + distance) % size) for i in range(size)]


def after(x, *earlier):
    return lax.optimization_barrier((x, *earlier))[0]


def shards(voltages, window, table):
    in_dev, frames, length = voltages.shape
    n_freq, n_col = lax.axis_size("freq"), lax.axis_size("col")
    n_in = in_dev // CHUNKS
    back = [(i + 1, i) for i in range(n_freq - 1)]
    row, col = lax.axis_index("row"), lax.axis_index("col")
    place = jnp.stack([row, col, (col + 3) % 4, (col + 1) % 4, (col + 2) % 4]).astype(jnp.int32)
    up, down = ring(n_col, 1), ring(n_col, -1)

    pieces = [voltages[:n_in]]
    rest = after(voltages, pieces[0])
    pieces += [rest[q * n_in : (q + 1) * n_in] for q in range(1, CHUNKS)]
    halos = []
    for q, waits in enumerate(((), (0,), (0,), (1,))):
        halos.append(lax.ppermute(after(pieces[q], *[halos[j] for j in waits]), "freq", back))
    sent, near, below, above, across, far = [[] for _ in range(6)]

    def front(q, *earlier):
        return channelize(n_in, voltages, q, halos[q], window, table, COPIES[q], earlier)

    def exchange(q, out):
        flat = out.reshape(n_freq * COPIES[q], *out.shape[2:])
        axes = "freq" if COPIES[q] == 1 else ("freq", "row")
        sent.append(lax.all_to_all(flat, axes, 0, 0, tiled=True).reshape(out.shape))

    def gather(q, *earlier):
        both = COPIES[q] == 2
        block = turn(sent[q], lambda place: place[0] if both else 0, place, earlier)
        near.append(block)
        free = after(block, *below[-1:], *above[-1:], *(across[q - 2] if q >= 2 else ()))
        below.append(lax.ppermute(free, "col", up))
        above.append(lax.ppermute(free, "col", down))
        part = block.shape[0] // PARTS
        if q < CHUNKS - 2:
            across.append([lax.ppermute(below[q][:part], "col", up), lax.ppermute(above[q][part:], "col", down)])

    def swap(q, *earlier):
        far.append(lax.ppermute(after(near[q], *earlier), "row", ring(2, 1)))

    def onward(q, j, *earlier):
        part = near[q].shape[0] // PARTS
        at = j * part
        source = below[q][at : at + part // 2], above[q][at + part // 2 : at + part]
        source = [after(x, *earlier) for x in source]
        return lax.ppermute(source[0], "col", up), lax.ppermute(source[1], "col", down)

    def cross(q, *earlier):
        far.append(turn(sent[q], lambda place: 1 - place[0], place, earlier))

    exchange(0, front(0))
    out = front(1)
    exchange(1, out)
    gather(0, out)
    swap(0, halos[-1])
    out = front(2, near[0])
    exchange(2, out)
    gather(1, out)
    out = front(3, near[1])
    exchange(3, out)
    gather(2, out, far[0])
    first = onward(2, 0)
    swap(1, sent[3])
    swap(2, sent[3])
    cross(3, near[2])
    gather(3, near[2], far[3])
    second = onward(3, 0, *first, far[1])
    third = onward(2, 1, *second, far[1])
    fourth = onward(3, 1, *second)
    across += [[jnp.concatenate(x, axis=0) for x in (first, third)], [jnp.concatenate(x, axis=0) for x in (second, fourth)]]
    outs = ()
    for part in range(PARTS):
        gathered = [near, below, above, [x[part] if isinstance(x, list) else x for x in across]]
        outs = correlate(place, gathered, far, part, PARTS, outs)
    return tuple(outs)


def solution(mesh):
    n_freq = mesh.shape["freq"]

    def run(voltages, window):
        table = jnp.asarray(dft_table(voltages.shape[2], n_freq))
        return jax.shard_map(
            shards,
            mesh=mesh,
            in_specs=(P(("row", "col"), "freq", None), P(), P()),
            out_specs=(P("freq", "row", "col"), P("freq", "row", "col")),
            check_vma=False,
        )(voltages, window, table)

    return run
```

time: 242 us -> 250 us (1.033); the launches traced: 241 us -> 245 us
  waiting for transfers between devices: 92 us -> 68.9 us
  starting transfers between devices: 63.2 us -> 73.8 us
  local copies, waits for them, and re-layouts: 8.79 us -> 16.8 us
  Pallas kernels: 75.7 us -> 81.4 us
  other arithmetic: 0 us -> 3.35 us
    all_to_all x4, waiting for transfers between devices: 30.4 us -> 10.1 us  [exchange(): sent.append(lax.all_to_all(flat, axes, 0, 0, tiled=True).reshape(out.shape))]
    slice x1 -> x10, local copies, waits for them, and re-layouts: 4.01 us -> 12.9 us  [the longest x1 3.5 us: shards(): pieces += [rest[q * n_in:(q + 1) * n_in] for q in range(1, CHUNKS)]]
    ppermute x24 -> x27, starting transfers between devices: 29.2 us -> 36.3 us  [the longest x4 8.57 us: onward(): lax.ppermute(source[1], 'col', down)]
    pallas_call x4 -> x5, Pallas kernels: 16.7 us -> 22.2 us  [turn(): pl.pallas_call(turn_kernel, grid_spec=pltpu.PrefetchScalarGridSpec(num_sc...]
    all_to_all x4, starting transfers between devices: 33.9 us -> 37.4 us  [exchange(): sent.append(lax.all_to_all(flat, axes, 0, 0, tiled=True).reshape(out.shape))]
    concatenate x0 -> x4, other arithmetic: none -> 3.35 us  [shards(): jnp.concatenate(x, axis=0)]
    ppermute x24 -> x27, waiting for transfers between devices: 61.6 us -> 58.8 us  [the longest x4 17.1 us: gather(): above.append(lax.ppermute(free, 'col', down))]
  transfers between devices with their start and end apart: 28 -> 31, of which waited for: 11 -> 13; matrix products, arithmetic and copies ran while one was open for 0% -> 6% of each run, Pallas kernels for 27% -> 29%
where the time goes in v3:
time: 250 us; the launch traced here: 245 us
  Pallas kernels  81.4 us (33%)
  starting transfers between devices  73.8 us (30%)
  waiting for transfers between devices  68.9 us (28%)
  local copies, waits for them, and re-layouts  16.8 us (7%)
  other arithmetic  3.35 us (1%)
    pallas_call x4, Pallas kernels, channelize(): pl.pallas_call(channelize_kernel, grid=(blocks,), in_specs=[pl.BlockSpec(...  40.1 us
    all_to_all x4, starting transfers between devices, exchange(): sent.append(lax.all_to_all(flat, axes, 0, 0, tiled=True).reshape(out.shape))  37.4 us
    pallas_call x5, Pallas kernels, turn(): pl.pallas_call(turn_kernel, grid_spec=pltpu.PrefetchScalarGridSpec(num_sc...  22.2 us
    pallas_call x2, Pallas kernels, correlate(): pl.pallas_call(functools.partial(correlate_kernel, chunks, 1.0 / depth),...  19 us
    ppermute x4, waiting for transfers between devices, gather(): above.append(lax.ppermute(free, 'col', down))  17.1 us
    ppermute x2, waiting for transfers between devices, gather(): lax.ppermute(above[q][part:], 'col', down)  16 us
    all_to_all x4, waiting for transfers between devices, exchange(): sent.append(lax.all_to_all(flat, axes, 0, 0, tiled=True).reshape(out.shape))  10.1 us
    ppermute x4, starting transfers between devices, onward(): lax.ppermute(source[1], 'col', down)  8.57 us
  transfers between devices with their start and end apart: 31, of which 13 were waited for; matrix products, arithmetic and copies ran while one was open for 6% of the time, Pallas kernels for 29%

profile of v3, /device:TPU:0, one launch (start us, length us, event | category | flops | bytes accessed | tf_op | source)
XLA Modules:
  0.0 245.2 jit_solution(8369898071958926923)
XLA Ops:
  0.6 1.3 slice.48
  2.0 1.3 collective-permute-start
  3.3 3.5 %fusion = (bf16[16,16,2048]{2,1,0:T(8,128)(2,1)}, bf16[16,16,2048]{2,1,0:T(8,128)(2,1)}, bf16[16,16,2048]{2,1,0:T(8,128)(2,1)S(1)}) fusion(bf16[64,16,2048]{2,1,0:T(8,128)(2,1)} %v_ref.7), kind=kLoop, calls=%fused_computation.4 | loop fusion | bytes 6291456 | tf_op jit(solution)/shard_map/slice | solution.py:207
  6.8 1.3 collective-permute-start.1
  8.1 10.0 %channelize.4 = bf16[16,1,16,16,128]{4,3,2,1,0:T(8,128)(2,1)} custom-call(bf16[64,16,2048]{2,1,0:T(8,128)(2,1)} %v_ref.7, bf16[16,16,2048]{2,1,0:T(8,128)(2,1)} %copy-done.12, f32[16,2048]{1,0:T(8,128)} %w_ref.7, bf16[4,2048,512]{2,1,0:T(8,128)(2,1)} %constant.37.clone.t_ref), custom_call_target="tpu_custom_call" | custom-call | flops 100000000 | bytes 131072 | tf_op jit(solution)/shard_map/channelize/pallas_call | solution.py:71
  18.1 18.4 %all-to-all-start = ((bf16[16,16,16,128]{3,2,1,0:T(8,128)(2,1)}), bf16[16,16,16,128]{3,2,1,0:T(8,128)(2,1)S(1)}, u32[]{:S(2)}, u32[]{:S(2)}) async-start(bf16[16,16,16,128]{3,2,1,0:T(8,128)(2,1)} %bitcast.18), calls=%async_computation | async-start | bytes 2097152 | tf_op jit(solution)/shard_map/all_to_all | solution.py:219
  36.5 1.3 collective-permute-start.2
  37.8 1.0 copy-done.11
  38.8 10.0 %channelize.5.refs_0_ = bf16[16,1,16,16,128]{4,3,2,1,0:T(8,128)(2,1)} custom-call(bf16[64,16,2048]{2,1,0:T(8,128)(2,1)} %v_ref.7, bf16[16,16,2048]{2,1,0:T(8,128)(2,1)} %copy-done.11, f32[16,2048]{1,0:T(8,128)} %w_ref.7, bf16[4,2048,512]{2,1,0:T(8,128)(2,1)} %constant.37.clone.t_ref), custom_call_target="tpu_custom_call" | custom-call | flops 100000000 | bytes 131072 | tf_op jit(solution)/shard_map/channelize/pallas_call | solution.py:71
  48.7 4.4 %all-to-all-done = bf16[16,16,16,128]{3,2,1,0:T(8,128)(2,1)S(1)} async-done(((bf16[16,16,16,128]{3,2,1,0:T(8,128)(2,1)}), bf16[16,16,16,128]{3,2,1,0:T(8,128)(2,1)S(1)}, u32[]{:S(2)}, u32[]{:S(2)}) %all-to-all-start) | async-done | bytes 1048608 | tf_op jit(solution)/shard_map/all_to_all | solution.py:219
  53.1 4.3 %all-to-all-start.1 = ((bf16[16,16,16,128]{3,2,1,0:T(8,128)(2,1)}), bf16[16,16,16,128]{3,2,1,0:T(8,128)(2,1)}, u32[]{:S(2)}, u32[]{:S(2)}) async-start(bf16[16,16,16,128]{3,2,1,0:T(8,128)(2,1)} %bitcast.16), calls=%async_computation.1 | async-start | bytes 2097152 | tf_op jit(solution)/shard_map/all_to_all | solution.py:219
  57.5 1.3 collective-permute-start.3
  58.8 0.6 stack.23.place
  59.4 4.4 %turn.5.refs_0_ = bf16[64,32,256]{2,1,0:T(8,128)(2,1)} custom-call(s32[5]{0:T(128)} %stack.23.place, bf16[16,1,16,16,128]{4,3,2,1,0:T(8,128)(2,1)} %bitcast.19, bf16[16,1,16,16,128]{4,3,2,1,0:T(8,128)(2,1)} %channelize.5.refs_0_), custom_call_target="tpu_custom_call" | custom-call | flops 100000000 | bytes 131072 | tf_op jit(solution)/shard_map/turn/pallas_call | solution.py:112
  63.8 4.0 %collective-permute-start.6 = (bf16[64,32,256]{2,1,0:T(8,128)(2,1)}, bf16[64,32,256]{2,1,0:T(8,128)(2,1)S(1)}, u32[]{:S(2)}, u32[]{:S(2)}) collective-permute-start(bf16[64,32,256]{2,1,0:T(8,128)(2,1)} %turn.5.refs_0_), channel_id=1, source_target_pairs={{0,3},{1,0},{2,1},{3,2},{4,7},{5,4},{6,5},{7,6},{8,11},{9,8},{10,9... | collective-permute-start | bytes 3145736 | tf_op jit(solution)/shard_map/ppermute | solution.py:227
  67.9 10.0 %channelize.6.refs_0_ = bf16[16,1,16,16,128]{4,3,2,1,0:T(8,128)(2,1)} custom-call(bf16[64,16,2048]{2,1,0:T(8,128)(2,1)} %v_ref.7, bf16[16,16,2048]{2,1,0:T(8,128)(2,1)} %collective-permute-done.2.h_ref, f32[16,2048]{1,0:T(8,128)} %w_ref.7, bf16[4,2048,512]{2,1,0:T(8,128)(2,1)} %constant.37.clone.t_ref, bf16[64,32,256]{2,1,0:T(8,128)(2,1)} %turn.5.refs_0_), custom_call_target="tpu_custom_call" | custom-call | flops 100000000 | bytes 131072 | tf_op jit(solution)/shard_map/channelize/pallas_call | solution.py:71
  77.8 6.8 %all-to-all-start.2 = ((bf16[16,16,16,128]{3,2,1,0:T(8,128)(2,1)}), bf16[16,16,16,128]{3,2,1,0:T(8,128)(2,1)}, u32[]{:S(2)}, u32[]{:S(2)}) async-start(bf16[16,16,16,128]{3,2,1,0:T(8,128)(2,1)} %bitcast.17), calls=%async_computation.2 | async-start | bytes 2097152 | tf_op jit(solution)/shard_map/all_to_all | solution.py:219
  84.7 2.8 %collective-permute-start.4 = (bf16[64,32,256]{2,1,0:T(8,128)(2,1)S(1)}, bf16[64,32,256]{2,1,0:T(8,128)(2,1)}, u32[]{:S(2)}, u32[]{:S(2)}) collective-permute-start(bf16[64,32,256]{2,1,0:T(8,128)(2,1)S(1)} %copy-done.3), channel_id=1, source_target_pairs={{0,4},{4,0},{1,5},{5,1},{2,6},{6,2},{3,7},{7,3},{8,12},{12,8},{9,1... | collective-permute-start | bytes 3145736 | tf_op jit(solution)/shard_map/ppermute | solution.py:233
  87.5 4.4 %turn.6.refs_0_.refs_1_ = bf16[64,32,256]{2,1,0:T(8,128)(2,1)} custom-call(s32[5]{0:T(128)} %stack.23.place, bf16[16,1,16,16,128]{4,3,2,1,0:T(8,128)(2,1)} %bitcast.8.x_ref, bf16[16,1,16,16,128]{4,3,2,1,0:T(8,128)(2,1)} %channelize.6.refs_0_), custom_call_target="tpu_custom_call" | custom-call | flops 100000000 | bytes 131072 | tf_op jit(solution)/shard_map/turn/pallas_call | solution.py:112
  91.9 3.3 %collective-permute-done.5.refs_4_ = bf16[64,32,256]{2,1,0:T(8,128)(2,1)S(1)} collective-permute-done((bf16[64,32,256]{2,1,0:T(8,128)(2,1)}, bf16[64,32,256]{2,1,0:T(8,128)(2,1)S(1)}, u32[]{:S(2)}, u32[]{:S(2)}) %collective-permute-start.5) | collective-permute-done | bytes 1048608 | tf_op jit(solution)/shard_map/ppermute | solution.py:226
  95.2 2.0 collective-permute-start.7
  97.2 10.2 %channelize.7.refs_0_ = bf16[16,2,16,16,128]{4,3,2,1,0:T(8,128)(2,1)} custom-call(bf16[64,16,2048]{2,1,0:T(8,128)(2,1)} %v_ref.7, bf16[16,16,2048]{2,1,0:T(8,128)(2,1)} %collective-permute-done.3.h_ref, f32[16,2048]{1,0:T(8,128)} %w_ref.7, bf16[4,2048,512]{2,1,0:T(8,128)(2,1)} %constant.37.clone.t_ref, bf16[64,32,256]{2,1,0:T(8,128)(2,1)} %turn.6.refs_0_.refs_1_), custom_call_target="tpu_custom_call" | custom-call | flops 100000000 | bytes 131072 | tf_op jit(solution)/shard_map/channelize/pallas_call | solution.py:71
  107.4 7.9 %all-to-all-start.3 = ((bf16[32,16,16,128]{3,2,1,0:T(8,128)(2,1)}), bf16[32,16,16,128]{3,2,1,0:T(8,128)(2,1)S(1)}, u32[]{:S(2)}, u32[]{:S(2)}) async-start(bf16[32,16,16,128]{3,2,1,0:T(8,128)(2,1)} %bitcast.15), calls=%async_computation.3 | async-start | bytes 4194304 | tf_op jit(solution)/shard_map/all_to_all | solution.py:219
  115.3 1.1 slice.65
  116.4 1.3 collective-permute-start.10
  117.7 1.1 slice.64
  118.8 0.9 collective-permute-start.9
  119.7 3.7 %collective-permute-done.4.refs_1_.refs_16_ = bf16[64,32,256]{2,1,0:T(8,128)(2,1)} collective-permute-done((bf16[64,32,256]{2,1,0:T(8,128)(2,1)S(1)}, bf16[64,32,256]{2,1,0:T(8,128)(2,1)}, u32[]{:S(2)}, u32[]{:S(2)}) %collective-permute-start.4) | collective-permute-done | bytes 1048608 | tf_op jit(solution)/shard_map/ppermute | solution.py:233
  123.3 4.5 %turn.7.refs_0_.refs_2_ = bf16[64,32,256]{2,1,0:T(8,128)(2,1)} custom-call(s32[5]{0:T(128)} %stack.23.place, bf16[16,1,16,16,128]{4,3,2,1,0:T(8,128)(2,1)} %bitcast.10.x_ref, bf16[16,2,16,16,128]{4,3,2,1,0:T(8,128)(2,1)} %channelize.7.refs_0_, bf16[64,32,256]{2,1,0:T(8,128)(2,1)} %collective-permute-done.4.refs_1_.refs_16_), custom_call_target="tpu_custom_call" | custom-call | flops 100000000 | bytes 131072 | tf_op jit(solution)/shard_map/turn/pallas_call | solution.py:112
  127.8 4.0 %collective-permute-done.10.refs_12_ = bf16[32,32,256]{2,1,0:T(8,128)(2,1)S(1)} collective-permute-done((bf16[32,32,256]{2,1,0:T(8,128)(2,1)S(1)}, bf16[32,32,256]{2,1,0:T(8,128)(2,1)S(1)}, u32[]{:S(2)}, u32[]{:S(2)}) %collective-permute-start.10) | collective-permute-done | bytes 524320 | tf_op jit(solution)/shard_map/ppermute | solution.py:230
  131.8 2.1 collective-permute-done.9.refs_12_
  134.2 2.0 collective-permute-start.11
  136.2 1.9 slice.67
  138.0 1.3 collective-permute-start.14
  139.3 1.9 slice.66
  141.2 0.7 collective-permute-start.13
  141.9 5.7 %all-to-all-done.3 = bf16[32,16,16,128]{3,2,1,0:T(8,128)(2,1)S(1)} async-done(((bf16[32,16,16,128]{3,2,1,0:T(8,128)(2,1)}), bf16[32,16,16,128]{3,2,1,0:T(8,128)(2,1)S(1)}, u32[]{:S(2)}, u32[]{:S(2)}) %all-to-all-start.3) | async-done | bytes 2097184 | tf_op jit(solution)/shard_map/all_to_all | solution.py:219
  147.7 1.3 copy-done.1
  149.0 4.4 %turn.8.refs_1_.refs_19_ = bf16[64,32,256]{2,1,0:T(8,128)(2,1)} custom-call(s32[5]{0:T(128)} %stack.23.place, bf16[16,2,16,16,128]{4,3,2,1,0:T(8,128)(2,1)} %bitcast.13, bf16[64,32,256]{2,1,0:T(8,128)(2,1)} %turn.7.refs_0_.refs_2_), custom_call_target="tpu_custom_call" | custom-call | flops 100000000 | bytes 131072 | tf_op jit(solution)/shard_map/turn/pallas_call | solution.py:112
  153.4 4.5 %turn.9.refs_3_ = bf16[64,32,256]{2,1,0:T(8,128)(2,1)} custom-call(s32[5]{0:T(128)} %stack.23.place, bf16[16,2,16,16,128]{4,3,2,1,0:T(8,128)(2,1)} %bitcast.14, bf16[64,32,256]{2,1,0:T(8,128)(2,1)} %turn.7.refs_0_.refs_2_, bf16[64,32,256]{2,1,0:T(8,128)(2,1)} %turn.8.refs_1_.refs_19_), custom_call_target="tpu_custom_call" | custom-call | flops 100000000 | bytes 131072 | tf_op jit(solution)/shard_map/turn/pallas_call | solution.py:112
  157.9 12.0 %collective-permute-done.14.refs_13_ = bf16[32,32,256]{2,1,0:T(8,128)(2,1)} collective-permute-done((bf16[32,32,256]{2,1,0:T(8,128)(2,1)}, bf16[32,32,256]{2,1,0:T(8,128)(2,1)}, u32[]{:S(2)}, u32[]{:S(2)}) %collective-permute-start.14) | collective-permute-done | bytes 524320 | tf_op jit(solution)/shard_map/ppermute | solution.py:230
  169.9 1.3 collective-permute-done.13.refs_13_
  171.5 3.0 %collective-permute-start.19 = (bf16[64,32,256]{2,1,0:T(8,128)(2,1)S(1)}, bf16[64,32,256]{2,1,0:T(8,128)(2,1)S(1)}, u32[]{:S(2)}, u32[]{:S(2)}) collective-permute-start(bf16[64,32,256]{2,1,0:T(8,128)(2,1)S(1)} %copy-done.2), channel_id=1, source_target_pairs={{0,4},{4,0},{1,5},{5,1},{2,6},{6,2},{3,7},{7,3},{8,12},{12,8},{9,1... | collective-permute-start | bytes 3145736 | tf_op jit(solution)/shard_map/ppermute | solution.py:233
  174.5 1.8 collective-permute-start.15
  176.3 0.5 collective-permute-start.26
  176.8 1.1 fusion.4
  177.8 1.6 collective-permute-start.18
  179.4 1.1 fusion.3
  180.5 17.1 %collective-permute-done.16.refs_11_ = bf16[64,32,256]{2,1,0:T(8,128)(2,1)S(1)} collective-permute-done((bf16[64,32,256]{2,1,0:T(8,128)(2,1)}, bf16[64,32,256]{2,1,0:T(8,128)(2,1)S(1)}, u32[]{:S(2)}, u32[]{:S(2)}) %collective-permute-start.16) | collective-permute-done | bytes 1048608 | tf_op jit(solution)/shard_map/ppermute | solution.py:227
  197.7 2.6 %collective-permute-done.18 = bf16[16,32,256]{2,1,0:T(8,128)(2,1)S(1)} collective-permute-done((bf16[16,32,256]{2,1,0:T(8,128)(2,1)S(1)}, bf16[16,32,256]{2,1,0:T(8,128)(2,1)S(1)}, u32[]{:S(2)}, u32[]{:S(2)}) %collective-permute-start.18) | collective-permute-done | bytes 262176 | tf_op jit(solution)/shard_map/ppermute | solution.py:240
  200.3 4.8 %collective-permute-done.17 = bf16[16,32,256]{2,1,0:T(8,128)(2,1)S(1)} collective-permute-done((bf16[16,32,256]{2,1,0:T(8,128)(2,1)S(1)}, bf16[16,32,256]{2,1,0:T(8,128)(2,1)S(1)}, u32[]{:S(2)}, u32[]{:S(2)}) %collective-permute-start.17) | collective-permute-done | bytes 262176 | tf_op jit(solution)/shard_map/ppermute | solution.py:240
  205.1 1.0 collective-permute-start.21
  206.1 1.1 collective-permute-start.20
  207.2 4.3 %collective-permute-done.21 = bf16[16,32,256]{2,1,0:T(8,128)(2,1)S(1)} collective-permute-done((bf16[16,32,256]{2,1,0:T(8,128)(2,1)S(1)}, bf16[16,32,256]{2,1,0:T(8,128)(2,1)S(1)}, u32[]{:S(2)}, u32[]{:S(2)}) %collective-permute-start.21) | collective-permute-done | bytes 262176 | tf_op jit(solution)/shard_map/ppermute | solution.py:240
  211.6 3.7 %collective-permute-done.20 = bf16[16,32,256]{2,1,0:T(8,128)(2,1)S(1)} collective-permute-done((bf16[16,32,256]{2,1,0:T(8,128)(2,1)S(1)}, bf16[16,32,256]{2,1,0:T(8,128)(2,1)S(1)}, u32[]{:S(2)}, u32[]{:S(2)}) %collective-permute-start.20) | collective-permute-done | bytes 262176 | tf_op jit(solution)/shard_map/ppermute | solution.py:240
  215.7 2.8 %collective-permute-start.23 = (bf16[16,32,256]{2,1,0:T(8,128)(2,1)S(1)}, bf16[16,32,256]{2,1,0:T(8,128)(2,1)S(1)}, u32[]{:S(2)}, u32[]{:S(2)}) collective-permute-start(bf16[16,32,256]{2,1,0:T(8,128)(2,1)S(1)} %get-tuple-element.32), channel_id=1, source_target_pairs={{0,3},{1,0},{2,1},{3,2},{4,7},{5,4},{6,5},{7,6},{8,11},{9,8},{10,9... | collective-permute-start | bytes 786440 | tf_op jit(solution)/shard_map/ppermute | solution.py:240
  218.5 3.2 %collective-permute-start.25 = (bf16[16,32,256]{2,1,0:T(8,128)(2,1)S(1)}, bf16[16,32,256]{2,1,0:T(8,128)(2,1)S(1)}, u32[]{:S(2)}, u32[]{:S(2)}) collective-permute-start(bf16[16,32,256]{2,1,0:T(8,128)(2,1)S(1)} %get-tuple-element.34), channel_id=1, source_target_pairs={{0,3},{1,0},{2,1},{3,2},{4,7},{5,4},{6,5},{7,6},{8,11},{9,8},{10,9... | collective-permute-start | bytes 786440 | tf_op jit(solution)/shard_map/ppermute | solution.py:240
  221.7 0.8 pad_maximum_fusion.2.refs_14_
  222.6 0.8 pad_maximum_fusion.3.refs_15_
  223.4 1.0 copy-done.10
  224.4 9.5 %correlate.2 = (f32[64,256,128]{2,1,0:T(8,128)}, f32[64,256,128]{2,1,0:T(8,128)}) custom-call(s32[5]{0:T(128)} %stack.23.place, bf16[64,32,256]{2,1,0:T(8,128)(2,1)} %turn.5.refs_0_, bf16[64,32,256]{2,1,0:T(8,128)(2,1)} %turn.6.refs_0_.refs_1_, bf16[64,32,256]{2,1,0:T(8,128)(2,1)} %turn.7.refs_0_.refs_2_, bf16[64,32,256]{2,1,0:T(8,128)(2,1)} %turn.9.refs_3_, ...), custom_call_target="tpu_custom_call" | custom-call | flops 100000000 | bytes 131072 | tf_op jit(solution)/shard_map/correlate/pallas_call | solution.py:171
  233.9 0.8 pad_maximum_fusion.refs_14_
  234.7 0.8 pad_maximum_fusion.1.refs_15_
  235.6 9.5 %correlate.3 = (f32[64,256,128]{2,1,0:T(8,128)}, f32[64,256,128]{2,1,0:T(8,128)}) custom-call(s32[5]{0:T(128)} %stack.23.place, bf16[64,32,256]{2,1,0:T(8,128)(2,1)} %turn.5.refs_0_, bf16[64,32,256]{2,1,0:T(8,128)(2,1)} %turn.6.refs_0_.refs_1_, bf16[64,32,256]{2,1,0:T(8,128)(2,1)} %turn.7.refs_0_.refs_2_, ...), custom_call_target="tpu_custom_call", output_to_operand_aliasing={{0}: (21, {}), {1}: (22, {})} | custom-call | flops 100000000 | bytes 131072 | tf_op jit(solution)/shard_map/correlate/pallas_call | solution.py:171
  (54 shorter events, 1.3 us)
Async XLA Ops:
  2.0 4.8 %collective-permute-start = (bf16[16,16,2048]{2,1,0:T(8,128)(2,1)S(1)}, bf16[16,16,2048]{2,1,0:T(8,128)(2,1)S(1)}, u32[]{:S(2)}, u32[]{:S(2)}) collective-permute-start(bf16[16,16,2048]{2,1,0:T(8,128)(2,1)S(1)} %slice.48), channel_id=1, source_target_pairs={{8,0},{16,8},{24,16},{32,24},{40,32},{48,40},{56,48},{64,56},{72,6... | collective-permute-start | bytes 3145736 | tf_op jit(solution)/shard_map/ppermute | solution.py:210
  6.8 1.3 copy-start.12
  6.8 31.0 %collective-permute-start.1 = (bf16[16,16,2048]{2,1,0:T(8,128)(2,1)S(1)}, bf16[16,16,2048]{2,1,0:T(8,128)(2,1)S(1)}, u32[]{:S(2)}, u32[]{:S(2)}) collective-permute-start(bf16[16,16,2048]{2,1,0:T(8,128)(2,1)S(1)} %get-tuple-element.21), channel_id=1, source_target_pairs={{8,0},{16,8},{24,16},{32,24},{40,32},{48,40},{56,48},{64,56},{72,6... | collective-permute-start | bytes 3145736 | tf_op jit(solution)/shard_map/ppermute | solution.py:210
  18.1 35.0 %all-to-all-start = ((bf16[16,16,16,128]{3,2,1,0:T(8,128)(2,1)}), bf16[16,16,16,128]{3,2,1,0:T(8,128)(2,1)S(1)}, u32[]{:S(2)}, u32[]{:S(2)}) async-start(bf16[16,16,16,128]{3,2,1,0:T(8,128)(2,1)} %bitcast.18), calls=%async_computation | async-start | bytes 2097152 | tf_op jit(solution)/shard_map/all_to_all | solution.py:219
  36.5 31.4 %collective-permute-start.2 = (bf16[16,16,2048]{2,1,0:T(8,128)(2,1)}, bf16[16,16,2048]{2,1,0:T(8,128)(2,1)}, u32[]{:S(2)}, u32[]{:S(2)}) collective-permute-start(bf16[16,16,2048]{2,1,0:T(8,128)(2,1)} %get-tuple-element.22), channel_id=1, source_target_pairs={{8,0},{16,8},{24,16},{32,24},{40,32},{48,40},{56,48},{64,56},{72,6... | collective-permute-start | bytes 3145736 | tf_op jit(solution)/shard_map/ppermute | solution.py:210
  37.8 1.0 copy-start.11
  53.1 6.3 %copy-start.8 = (bf16[16,16,16,128]{3,2,1,0:T(8,128)(2,1)}, bf16[16,16,16,128]{3,2,1,0:T(8,128)(2,1)S(1)}, u32[]{:S(2)}) copy-start(bf16[16,16,16,128]{3,2,1,0:T(8,128)(2,1)S(1)} %all-to-all-done) | copy-start | bytes 3145732
  53.1 24.8 %all-to-all-start.1 = ((bf16[16,16,16,128]{3,2,1,0:T(8,128)(2,1)}), bf16[16,16,16,128]{3,2,1,0:T(8,128)(2,1)}, u32[]{:S(2)}, u32[]{:S(2)}) async-start(bf16[16,16,16,128]{3,2,1,0:T(8,128)(2,1)} %bitcast.16), calls=%async_computation.1 | async-start | bytes 2097152 | tf_op jit(solution)/shard_map/all_to_all | solution.py:219
  57.5 27.2 %collective-permute-start.3 = (bf16[16,16,2048]{2,1,0:T(8,128)(2,1)}, bf16[16,16,2048]{2,1,0:T(8,128)(2,1)}, u32[]{:S(2)}, u32[]{:S(2)}) collective-permute-start(bf16[16,16,2048]{2,1,0:T(8,128)(2,1)} %get-tuple-element.23), channel_id=1, source_target_pairs={{8,0},{16,8},{24,16},{32,24},{40,32},{48,40},{56,48},{64,56},{72,6... | collective-permute-start | bytes 3145736 | tf_op jit(solution)/shard_map/ppermute | solution.py:210
  63.8 20.9 %copy-start.3 = (bf16[64,32,256]{2,1,0:T(8,128)(2,1)S(1)}, bf16[64,32,256]{2,1,0:T(8,128)(2,1)}, u32[]{:S(2)}) copy-start(bf16[64,32,256]{2,1,0:T(8,128)(2,1)} %turn.5.refs_0_) | copy-start | bytes 3145732
  63.8 28.1 %collective-permute-start.6 = (bf16[64,32,256]{2,1,0:T(8,128)(2,1)}, bf16[64,32,256]{2,1,0:T(8,128)(2,1)S(1)}, u32[]{:S(2)}, u32[]{:S(2)}) collective-permute-start(bf16[64,32,256]{2,1,0:T(8,128)(2,1)} %turn.5.refs_0_), channel_id=1, source_target_pairs={{0,3},{1,0},{2,1},{3,2},{4,7},{5,4},{6,5},{7,6},{8,11},{9,8},{10,9... | collective-permute-start | bytes 3145736 | tf_op jit(solution)/shard_map/ppermute | solution.py:227
  67.9 27.3 %collective-permute-start.5 = (bf16[64,32,256]{2,1,0:T(8,128)(2,1)}, bf16[64,32,256]{2,1,0:T(8,128)(2,1)S(1)}, u32[]{:S(2)}, u32[]{:S(2)}) collective-permute-start(bf16[64,32,256]{2,1,0:T(8,128)(2,1)} %turn.5.refs_0_), channel_id=1, source_target_pairs={{0,1},{1,2},{2,3},{3,0},{4,5},{5,6},{6,7},{7,4},{8,9},{9,10},{10,1... | collective-permute-start | bytes 3145736 | tf_op jit(solution)/shard_map/ppermute | solution.py:226
  77.8 29.6 %all-to-all-start.2 = ((bf16[16,16,16,128]{3,2,1,0:T(8,128)(2,1)}), bf16[16,16,16,128]{3,2,1,0:T(8,128)(2,1)}, u32[]{:S(2)}, u32[]{:S(2)}) async-start(bf16[16,16,16,128]{3,2,1,0:T(8,128)(2,1)} %bitcast.17), calls=%async_computation.2 | async-start | bytes 2097152 | tf_op jit(solution)/shard_map/all_to_all | solution.py:219
  84.7 38.6 %collective-permute-start.4 = (bf16[64,32,256]{2,1,0:T(8,128)(2,1)S(1)}, bf16[64,32,256]{2,1,0:T(8,128)(2,1)}, u32[]{:S(2)}, u32[]{:S(2)}) collective-permute-start(bf16[64,32,256]{2,1,0:T(8,128)(2,1)S(1)} %copy-done.3), channel_id=1, source_target_pairs={{0,4},{4,0},{1,5},{5,1},{2,6},{6,2},{3,7},{7,3},{8,12},{12,8},{9,1... | collective-permute-start | bytes 3145736 | tf_op jit(solution)/shard_map/ppermute | solution.py:233
  91.9 15.5 %copy-start.4 = (bf16[64,32,256]{2,1,0:T(8,128)(2,1)}, bf16[64,32,256]{2,1,0:T(8,128)(2,1)S(1)}, u32[]{:S(2)}) copy-start(bf16[64,32,256]{2,1,0:T(8,128)(2,1)S(1)} %collective-permute-done.6.refs_8_) | copy-start | bytes 3145732
  95.2 12.2 %copy-start.5 = (bf16[64,32,256]{2,1,0:T(8,128)(2,1)}, bf16[64,32,256]{2,1,0:T(8,128)(2,1)S(1)}, u32[]{:S(2)}) copy-start(bf16[64,32,256]{2,1,0:T(8,128)(2,1)S(1)} %collective-permute-done.5.refs_4_) | copy-start | bytes 3145732
  95.2 38.7 %collective-permute-start.8 = (bf16[64,32,256]{2,1,0:T(8,128)(2,1)}, bf16[64,32,256]{2,1,0:T(8,128)(2,1)}, u32[]{:S(2)}, u32[]{:S(2)}) collective-permute-start(bf16[64,32,256]{2,1,0:T(8,128)(2,1)} %turn.6.refs_0_.refs_1_), channel_id=1, source_target_pairs={{0,3},{1,0},{2,1},{3,2},{4,7},{5,4},{6,5},{7,6},{8,11},{9,8},{10,9... | collective-permute-start | bytes 3145736 | tf_op jit(solution)/shard_map/ppermute | solution.py:227
  95.2 38.7 %collective-permute-start.7 = (bf16[64,32,256]{2,1,0:T(8,128)(2,1)}, bf16[64,32,256]{2,1,0:T(8,128)(2,1)}, u32[]{:S(2)}, u32[]{:S(2)}) collective-permute-start(bf16[64,32,256]{2,1,0:T(8,128)(2,1)} %turn.6.refs_0_.refs_1_), channel_id=1, source_target_pairs={{0,1},{1,2},{2,3},{3,0},{4,5},{5,6},{6,7},{7,4},{8,9},{9,10},{10,1... | collective-permute-start | bytes 3145736 | tf_op jit(solution)/shard_map/ppermute | solution.py:226
  107.4 40.2 %all-to-all-start.3 = ((bf16[32,16,16,128]{3,2,1,0:T(8,128)(2,1)}), bf16[32,16,16,128]{3,2,1,0:T(8,128)(2,1)S(1)}, u32[]{:S(2)}, u32[]{:S(2)}) async-start(bf16[32,16,16,128]{3,2,1,0:T(8,128)(2,1)} %bitcast.15), calls=%async_computation.3 | async-start | bytes 4194304 | tf_op jit(solution)/shard_map/all_to_all | solution.py:219
  116.4 15.4 %collective-permute-start.10 = (bf16[32,32,256]{2,1,0:T(8,128)(2,1)S(1)}, bf16[32,32,256]{2,1,0:T(8,128)(2,1)S(1)}, u32[]{:S(2)}, u32[]{:S(2)}) collective-permute-start(bf16[32,32,256]{2,1,0:T(8,128)(2,1)S(1)} %slice.65), channel_id=1, source_target_pairs={{0,3},{1,0},{2,1},{3,2},{4,7},{5,4},{6,5},{7,6},{8,11},{9,8},{10,9... | collective-permute-start | bytes 1572872 | tf_op jit(solution)/shard_map/ppermute | solution.py:230
  118.8 15.1 %collective-permute-start.9 = (bf16[32,32,256]{2,1,0:T(8,128)(2,1)S(1)}, bf16[32,32,256]{2,1,0:T(8,128)(2,1)S(1)}, u32[]{:S(2)}, u32[]{:S(2)}) collective-permute-start(bf16[32,32,256]{2,1,0:T(8,128)(2,1)S(1)} %slice.64), channel_id=1, source_target_pairs={{0,1},{1,2},{2,3},{3,0},{4,5},{5,6},{6,7},{7,4},{8,9},{9,10},{10,1... | collective-permute-start | bytes 1572872 | tf_op jit(solution)/shard_map/ppermute | solution.py:230
  127.8 48.5 %copy-start = (bf16[64,32,256]{2,1,0:T(8,128)(2,1)S(1)}, bf16[64,32,256]{2,1,0:T(8,128)(2,1)}, u32[]{:S(2)}) copy-start(bf16[64,32,256]{2,1,0:T(8,128)(2,1)} %turn.7.refs_0_.refs_2_) | copy-start | bytes 3145732
  131.8 9.4 %copy-start.13 = (bf16[32,32,256]{2,1,0:T(8,128)(2,1)}, bf16[32,32,256]{2,1,0:T(8,128)(2,1)S(1)}, u32[]{:S(2)}) copy-start(bf16[32,32,256]{2,1,0:T(8,128)(2,1)S(1)} %collective-permute-done.10.refs_12_) | copy-start | bytes 1572868
  133.9 7.3 %copy-start.14 = (bf16[32,32,256]{2,1,0:T(8,128)(2,1)}, bf16[32,32,256]{2,1,0:T(8,128)(2,1)S(1)}, u32[]{:S(2)}) copy-start(bf16[32,32,256]{2,1,0:T(8,128)(2,1)S(1)} %collective-permute-done.9.refs_12_) | copy-start | bytes 1572868
  133.9 37.3 %collective-permute-start.12 = (bf16[64,32,256]{2,1,0:T(8,128)(2,1)}, bf16[64,32,256]{2,1,0:T(8,128)(2,1)}, u32[]{:S(2)}, u32[]{:S(2)}) collective-permute-start(bf16[64,32,256]{2,1,0:T(8,128)(2,1)} %turn.7.refs_0_.refs_2_), channel_id=1, source_target_pairs={{0,3},{1,0},{2,1},{3,2},{4,7},{5,4},{6,5},{7,6},{8,11},{9,8},{10,9... | collective-permute-start | bytes 3145736 | tf_op jit(solution)/shard_map/ppermute | solution.py:227
  134.2 37.0 %collective-permute-start.11 = (bf16[64,32,256]{2,1,0:T(8,128)(2,1)}, bf16[64,32,256]{2,1,0:T(8,128)(2,1)}, u32[]{:S(2)}, u32[]{:S(2)}) collective-permute-start(bf16[64,32,256]{2,1,0:T(8,128)(2,1)} %turn.7.refs_0_.refs_2_), channel_id=1, source_target_pairs={{0,1},{1,2},{2,3},{3,0},{4,5},{5,6},{6,7},{7,4},{8,9},{9,10},{10,1... | collective-permute-start | bytes 3145736 | tf_op jit(solution)/shard_map/ppermute | solution.py:226
  138.0 31.9 %collective-permute-start.14 = (bf16[32,32,256]{2,1,0:T(8,128)(2,1)}, bf16[32,32,256]{2,1,0:T(8,128)(2,1)}, u32[]{:S(2)}, u32[]{:S(2)}) collective-permute-start(bf16[32,32,256]{2,1,0:T(8,128)(2,1)} %slice.67), channel_id=1, source_target_pairs={{0,3},{1,0},{2,1},{3,2},{4,7},{5,4},{6,5},{7,6},{8,11},{9,8},{10,9... | collective-permute-start | bytes 1572872 | tf_op jit(solution)/shard_map/ppermute | solution.py:230
  141.2 30.0 %collective-permute-start.13 = (bf16[32,32,256]{2,1,0:T(8,128)(2,1)}, bf16[32,32,256]{2,1,0:T(8,128)(2,1)}, u32[]{:S(2)}, u32[]{:S(2)}) collective-permute-start(bf16[32,32,256]{2,1,0:T(8,128)(2,1)} %slice.66), channel_id=1, source_target_pairs={{0,1},{1,2},{2,3},{3,0},{4,5},{5,6},{6,7},{7,4},{8,9},{9,10},{10,1... | collective-permute-start | bytes 1572872 | tf_op jit(solution)/shard_map/ppermute | solution.py:230
  147.7 1.3 copy-start.1
  147.7 23.8 %copy-start.2 = (bf16[64,32,256]{2,1,0:T(8,128)(2,1)S(1)}, bf16[64,32,256]{2,1,0:T(8,128)(2,1)}, u32[]{:S(2)}) copy-start(bf16[64,32,256]{2,1,0:T(8,128)(2,1)} %turn.6.refs_0_.refs_1_) | copy-start | bytes 3145732
  171.2 26.3 %collective-permute-start.16 = (bf16[64,32,256]{2,1,0:T(8,128)(2,1)}, bf16[64,32,256]{2,1,0:T(8,128)(2,1)S(1)}, u32[]{:S(2)}, u32[]{:S(2)}) collective-permute-start(bf16[64,32,256]{2,1,0:T(8,128)(2,1)} %turn.9.refs_3_), channel_id=1, source_target_pairs={{0,3},{1,0},{2,1},{3,2},{4,7},{5,4},{6,5},{7,6},{8,11},{9,8},{10,9... | collective-permute-start | bytes 3145736 | tf_op jit(solution)/shard_map/ppermute | solution.py:227
  171.5 33.6 %collective-permute-start.19 = (bf16[64,32,256]{2,1,0:T(8,128)(2,1)S(1)}, bf16[64,32,256]{2,1,0:T(8,128)(2,1)S(1)}, u32[]{:S(2)}, u32[]{:S(2)}) collective-permute-start(bf16[64,32,256]{2,1,0:T(8,128)(2,1)S(1)} %copy-done.2), channel_id=1, source_target_pairs={{0,4},{4,0},{1,5},{5,1},{2,6},{6,2},{3,7},{7,3},{8,12},{12,8},{9,1... | collective-permute-start | bytes 3145736 | tf_op jit(solution)/shard_map/ppermute | solution.py:233
  174.5 31.6 %collective-permute-start.15 = (bf16[64,32,256]{2,1,0:T(8,128)(2,1)}, bf16[64,32,256]{2,1,0:T(8,128)(2,1)S(1)}, u32[]{:S(2)}, u32[]{:S(2)}) collective-permute-start(bf16[64,32,256]{2,1,0:T(8,128)(2,1)} %turn.9.refs_3_), channel_id=1, source_target_pairs={{0,1},{1,2},{2,3},{3,0},{4,5},{5,6},{6,7},{7,4},{8,9},{9,10},{10,1... | collective-permute-start | bytes 3145736 | tf_op jit(solution)/shard_map/ppermute | solution.py:226
  176.3 47.1 %collective-permute-start.26 = (bf16[64,32,256]{2,1,0:T(8,128)(2,1)S(1)}, bf16[64,32,256]{2,1,0:T(8,128)(2,1)S(1)}, u32[]{:S(2)}, u32[]{:S(2)}) collective-permute-start(bf16[64,32,256]{2,1,0:T(8,128)(2,1)S(1)} %copy-done), channel_id=1, source_target_pairs={{0,4},{4,0},{1,5},{5,1},{2,6},{6,2},{3,7},{7,3},{8,12},{12,8},{9,1... | collective-permute-start | bytes 3145736 | tf_op jit(solution)/shard_map/ppermute | solution.py:233
  177.8 22.5 %collective-permute-start.18 = (bf16[16,32,256]{2,1,0:T(8,128)(2,1)S(1)}, bf16[16,32,256]{2,1,0:T(8,128)(2,1)S(1)}, u32[]{:S(2)}, u32[]{:S(2)}) collective-permute-start(bf16[16,32,256]{2,1,0:T(8,128)(2,1)S(1)} %get-tuple-element.47), channel_id=1, source_target_pairs={{0,3},{1,0},{2,1},{3,2},{4,7},{5,4},{6,5},{7,6},{8,11},{9,8},{10,9... | collective-permute-start | bytes 786440 | tf_op jit(solution)/shard_map/ppermute | solution.py:240
  197.5 25.9 %copy-start.6 = (bf16[64,32,256]{2,1,0:T(8,128)(2,1)}, bf16[64,32,256]{2,1,0:T(8,128)(2,1)S(1)}, u32[]{:S(2)}) copy-start(bf16[64,32,256]{2,1,0:T(8,128)(2,1)S(1)} %collective-permute-done.16.refs_11_) | copy-start | bytes 3145732
  197.5 7.6 %collective-permute-start.17 = (bf16[16,32,256]{2,1,0:T(8,128)(2,1)S(1)}, bf16[16,32,256]{2,1,0:T(8,128)(2,1)S(1)}, u32[]{:S(2)}, u32[]{:S(2)}) collective-permute-start(bf16[16,32,256]{2,1,0:T(8,128)(2,1)S(1)} %get-tuple-element.46), channel_id=1, source_target_pairs={{0,1},{1,2},{2,3},{3,0},{4,5},{5,6},{6,7},{7,4},{8,9},{9,10},{10,1... | collective-permute-start | bytes 786440 | tf_op jit(solution)/shard_map/ppermute | solution.py:240
  205.1 18.3 %copy-start.9 = (bf16[64,32,256]{2,1,0:T(8,128)(2,1)}, bf16[64,32,256]{2,1,0:T(8,128)(2,1)S(1)}, u32[]{:S(2)}) copy-start(bf16[64,32,256]{2,1,0:T(8,128)(2,1)S(1)} %collective-permute-done.19.refs_17_) | copy-start | bytes 3145732
  205.1 6.5 %collective-permute-start.21 = (bf16[16,32,256]{2,1,0:T(8,128)(2,1)S(1)}, bf16[16,32,256]{2,1,0:T(8,128)(2,1)S(1)}, u32[]{:S(2)}, u32[]{:S(2)}) collective-permute-start(bf16[16,32,256]{2,1,0:T(8,128)(2,1)S(1)} %get-tuple-element.30), channel_id=1, source_target_pairs={{0,3},{1,0},{2,1},{3,2},{4,7},{5,4},{6,5},{7,6},{8,11},{9,8},{10,9... | collective-permute-start | bytes 786440 | tf_op jit(solution)/shard_map/ppermute | solution.py:240
  206.1 17.3 %copy-start.7 = (bf16[64,32,256]{2,1,0:T(8,128)(2,1)}, bf16[64,32,256]{2,1,0:T(8,128)(2,1)S(1)}, u32[]{:S(2)}) copy-start(bf16[64,32,256]{2,1,0:T(8,128)(2,1)S(1)} %collective-permute-done.15.refs_7_) | copy-start | bytes 3145732
  206.1 9.1 %collective-permute-start.20 = (bf16[16,32,256]{2,1,0:T(8,128)(2,1)S(1)}, bf16[16,32,256]{2,1,0:T(8,128)(2,1)S(1)}, u32[]{:S(2)}, u32[]{:S(2)}) collective-permute-start(bf16[16,32,256]{2,1,0:T(8,128)(2,1)S(1)} %get-tuple-element.29), channel_id=1, source_target_pairs={{0,1},{1,2},{2,3},{3,0},{4,5},{5,6},{6,7},{7,4},{8,9},{9,10},{10,1... | collective-permute-start | bytes 786440 | tf_op jit(solution)/shard_map/ppermute | solution.py:240
  215.2 18.6 %collective-permute-start.22 = (bf16[16,32,256]{2,1,0:T(8,128)(2,1)S(1)}, bf16[16,32,256]{2,1,0:T(8,128)(2,1)S(1)}, u32[]{:S(2)}, u32[]{:S(2)}) collective-permute-start(bf16[16,32,256]{2,1,0:T(8,128)(2,1)S(1)} %get-tuple-element.31), channel_id=1, source_target_pairs={{0,1},{1,2},{2,3},{3,0},{4,5},{5,6},{6,7},{7,4},{8,9},{9,10},{10,1... | collective-permute-start | bytes 786440 | tf_op jit(solution)/shard_map/ppermute | solution.py:240
  215.7 18.2 %collective-permute-start.23 = (bf16[16,32,256]{2,1,0:T(8,128)(2,1)S(1)}, bf16[16,32,256]{2,1,0:T(8,128)(2,1)S(1)}, u32[]{:S(2)}, u32[]{:S(2)}) collective-permute-start(bf16[16,32,256]{2,1,0:T(8,128)(2,1)S(1)} %get-tuple-element.32), channel_id=1, source_target_pairs={{0,3},{1,0},{2,1},{3,2},{4,7},{5,4},{6,5},{7,6},{8,11},{9,8},{10,9... | collective-permute-start | bytes 786440 | tf_op jit(solution)/shard_map/ppermute | solution.py:240
  218.5 16.3 %collective-permute-start.24 = (bf16[16,32,256]{2,1,0:T(8,128)(2,1)S(1)}, bf16[16,32,256]{2,1,0:T(8,128)(2,1)S(1)}, u32[]{:S(2)}, u32[]{:S(2)}) collective-permute-start(bf16[16,32,256]{2,1,0:T(8,128)(2,1)S(1)} %get-tuple-element.33), channel_id=1, source_target_pairs={{0,1},{1,2},{2,3},{3,0},{4,5},{5,6},{6,7},{7,4},{8,9},{9,10},{10,1... | collective-permute-start | bytes 786440 | tf_op jit(solution)/shard_map/ppermute | solution.py:240
  218.5 16.3 %collective-permute-start.25 = (bf16[16,32,256]{2,1,0:T(8,128)(2,1)S(1)}, bf16[16,32,256]{2,1,0:T(8,128)(2,1)S(1)}, u32[]{:S(2)}, u32[]{:S(2)}) collective-permute-start(bf16[16,32,256]{2,1,0:T(8,128)(2,1)S(1)} %get-tuple-element.34), channel_id=1, source_target_pairs={{0,3},{1,0},{2,1},{3,2},{4,7},{5,4},{6,5},{7,6},{8,11},{9,8},{10,9... | collective-permute-start | bytes 786440 | tf_op jit(solution)/shard_map/ppermute | solution.py:240
  223.4 1.0 copy-start.10
